TPU v7x, 32 devices: a whole 2x2x4 slice. The times are simulated.
32 devices in a mesh: grp: 4 (over z), shard: 8 (over y, x, core).
Axes of the slice: x: 2, y: 2, z: 4, core: 2. Of those that a mesh axis runs over, the one named last changes fastest.
Arguments:
- patches: bfloat16 [8192, 16], P(('grp', 'shard')), may hold values from -6 to 6
- noise: float32 [8192, 16], P(('grp', 'shard')), may hold values from -6 to 6
- timesteps: int32 [32], P(('grp', 'shard')), may hold values from 0 to 999
- labels: int32 [32], P(('grp', 'shard')), may hold values from 0 to 999
- assign: int32 [288], replicated, may hold values from 0 to 287, each once
- tile_master: float32 [288, 256, 256], P('shard'), may hold values from -0.1875 to 0.1875
- tile_bases: float32 [288, 2, 256, 256], P('shard'), may hold values from -1 to 1, as said below
- tile_moment: float32 [288, 256, 256], P('shard'), may hold values from -0.0007324219 to 0.0007324219
- tile_second: float32 [288, 256, 256], P('shard'), may hold values from 3e-10 to 1e-08
- row_master: float32 [4379, 1024], P(None, 'shard'), may hold values from -1.5 to 1.5
- row_moment: float32 [4379, 1024], P(None, 'shard'), may hold values from -0.0007324219 to 0.0007324219
- row_second: float32 [4379, 1024], P(None, 'shard'), may hold values from 3e-10 to 1e-08
Outputs:
- loss: float32 [], replicated
- grad_norm: float32 [], replicated
- act_rms: float32 [3], replicated
- new_tile_moment: float32 [288, 256, 256], P('shard')
- new_tile_second: float32 [288, 256, 256], P('shard')
- tile_update: float32 [288, 256, 256], P('shard')
- new_row_moment: float32 [4379, 1024], P(None, 'shard')
- new_row_second: float32 [4379, 1024], P(None, 'shard')
- row_update: float32 [4379, 1024], P(None, 'shard')
Inputs may be any that keep to these rules, and one draw needn't show every extreme that they name: assign is a permutation: each block stands in exactly one slot; slot s belongs to the owner s // 36. tile_bases[s, 0] and tile_bases[s, 1] are orthogonal matrices.
All inputs are finite; a program needn't handle non-finite values.
Results may differ from a plain program's by a relative error of at most 0.018.
Values may be sent and summed in bfloat16 or wider, within the bound.
A program may use at most 448 MiB of HBM per device.

v0:
```python
import functools
import math

import jax
import jax.numpy as jnp
from jax import lax
from jax.experimental import pallas as pl
from jax.experimental.pallas import tpu as pltpu
from jax.sharding import PartitionSpec as P

D = 1024
HEADS = 16
HD = 64
FF = 4096
NCLASS = 1000
FREQ = 256
PATCH_SIDE = 2
LAT = 32
BLK = 256
PATCH_DIM = 16
SEQ = 256

NB = D // BLK
HB = FF // BLK
QB = 3 * NB
ADA = NB * 6 * NB
BIG = NB * QB + NB * NB + 2 * NB * HB
AT_QKV, AT_OUT, AT_UP, AT_DOWN = 0, NB * QB, NB * QB + NB * NB, NB * QB + NB * NB + NB * HB
L_ATT, L_OUT, L_MLP, L_HID = 0, NB, 2 * NB, 3 * NB
R_QKV = 3 * NB + HB
R_OUT = R_QKV + QB
R_UP = R_OUT + NB
R_DOWN = R_UP + HB
ACTS = R_DOWN + NB
B_OUT, B_UP, B_DOWN = QB, QB + NB, QB + NB + HB
ROW_STEP = 128
ADAM_GROUP = 3
LANES = D // 128
NEAR = 64
NEAR_START = NCLASS + FREQ + 3 * D
N_PATCH, N_TIME1, N_TIME2, N_QUERY, N_VALUE, N_OUT, N_DOWN, N_ADA = range(2 * PATCH_DIM, 2 * PATCH_DIM + 8)
N_UP = N_ADA + 6
N_FINAL = N_UP + FF // D
NEAR_REAL = N_FINAL + 2
T_PATCH, T_OUT, T_DOWN, T_QUERY, T_VALUE, T_UP = range(2 * PATCH_DIM, 2 * PATCH_DIM + 6)
T_END = T_UP + FF // D
TOKEN_ROWS = 48

CAPS = (28, 30)
GROUPS, SHARDS = 4, 8
MESH_ID = pl.DeviceIdType.MESH

ln_eps = 1e-06
beta_one = 0.5
beta_two = 0.5
adam_eps = 1e-08
rate_step = 0.01
decay_rate = 0.1
clip_at = 0.25

f32 = jnp.float32
bf16 = jnp.bfloat16


def nn(left, right):
    return lax.dot_general(left, right, (((1,), (0,)), ((), ())), preferred_element_type=f32)


def nt(left, right):
    return lax.dot_general(left, right, (((1,), (1,)), ((), ())), preferred_element_type=f32)


def tn(left, right):
    return lax.dot_general(left, right, (((0,), (0,)), ((), ())), preferred_element_type=f32)


def wide(ref, at, count=ROW_STEP):
    return jnp.concatenate([ref[r, pl.ds(at, count), :] for r in range(NB)], axis=1)


def put(ref, base, at, value, count=ROW_STEP):
    for r in range(NB):
        ref[base + r, pl.ds(at, count), :] = value[:, r * BLK : (r + 1) * BLK].astype(ref.dtype)


def fold(value):
    return jnp.sum(value.reshape(-1, 8, value.shape[-1]), axis=0)


def normed(value):
    centred = value - jnp.mean(value, axis=-1, keepdims=True)
    spread = jnp.mean(centred * centred, axis=-1, keepdims=True)
    back = lax.rsqrt(spread + ln_eps)
    return centred * back, back


def over_rows(body):
    def step(i, unused):
        body(pl.multiple_of(i * ROW_STEP, ROW_STEP))
        return unused

    lax.fori_loop(0, SEQ // ROW_STEP, step, 0)


def over(count, body, together=2):
    def step(i, unused):
        body(i)
        return unused

    lax.fori_loop(0, count, step, 0, unroll=together)


def norm_back(grad, value, scale):
    norm, back = normed(value)
    inner = grad * (1.0 + scale)
    mean_one = jnp.mean(inner, axis=-1, keepdims=True)
    mean_two = jnp.mean(inner * norm, axis=-1, keepdims=True)
    return norm, (inner - mean_one - norm * mean_two) * back


def gelu_pair(value):
    root = math.sqrt(2.0 / math.pi)
    square = value * value
    bend = jnp.tanh(root * (value + 0.044715 * value * square))
    half = 0.5 * (1.0 + bend)
    slope = half + 0.5 * value * (1.0 - bend * bend) * root * (1.0 + 3 * 0.044715 * square)
    return value * half, slope


def block_body(
    loss_factor, place_ref, tiles_ref, patches_ref, noise_ref, spot_ref, near_ref, mods_ref,
    acts_ref, dmod_ref, ends_ref, stats_ref,
    w_ref, stream, middle, last, out_att, out_mlp, low_in, low_att, qkv, hid, slope, probs, flow, sums,
    near_wide, bias_ref, mod_ref, dbias_ref, w_sem,
):
    att_scale = HD ** (-0.5)
    cuts = (AT_QKV, AT_OUT, AT_UP, AT_DOWN, BIG)

    def fetch(b, sem):
        pltpu.make_async_copy(tiles_ref.at[place_ref[ADA + b]], w_ref.at[b], w_sem.at[sem]).start()

    for m in range(4):
        over(cuts[m + 1] - cuts[m], lambda b, m=m: fetch(cuts[m] + b, m))

    def arrived(m):
        span = pl.ds(cuts[m], cuts[m + 1] - cuts[m])
        pltpu.make_async_copy(tiles_ref.at[pl.ds(0, cuts[m + 1] - cuts[m])], w_ref.at[span], w_sem.at[m]).wait()

    def mod(i):
        return mod_ref[i : i + 1, :]

    near_wide[...] = near_ref[...].astype(f32)

    def row_block(row, r):
        return jnp.concatenate([near_wide[2 * r, row : row + 1, :], near_wide[2 * r + 1, row : row + 1, :]], axis=1)

    def near_block(row, r):
        span = slice(row, row + PATCH_DIM)
        return jnp.concatenate([near_ref[2 * r, span, :], near_ref[2 * r + 1, span, :]], axis=1)

    for r in range(NB):
        bias_ref[r] = row_block(N_QUERY, r)
        bias_ref[NB + r] = jnp.zeros((1, BLK), f32)
        bias_ref[2 * NB + r] = row_block(N_VALUE, r)
        bias_ref[B_OUT + r] = row_block(N_OUT, r)
        bias_ref[B_DOWN + r] = row_block(N_DOWN, r)
        for i in range(FF // D):
            bias_ref[B_UP + i * NB + r] = row_block(N_UP + i, r)
    for i in range(8):
        mod_ref[i : i + 1, :] = jnp.concatenate([mods_ref[i * LANES + o : i * LANES + o + 1, :] for o in range(LANES)], axis=1)

    lane = lax.broadcasted_iota(jnp.int32, (SEQ, 128), 1)
    lower = lane < HD
    halves = (lower, jnp.logical_not(lower))

    def masked(value, side):
        return jnp.where(halves[side], value, jnp.zeros_like(value))

    sums[...] = jnp.zeros_like(sums)
    S_SQ_END, S_SQ_ATT, S_SQ_MLP = 0, 1, 2
    S_DSH_A, S_DSC_A, S_DG_A, S_DSH_M, S_DSC_M, S_DG_M, S_DSH_F, S_DSC_F = range(3, 11)
    S_PATCH, S_OUT, S_DOWN = 11, 12, 13

    def collect(which, value):
        sums[which] = sums[which] + fold(value)

    patches = patches_ref[...]
    side = LAT // PATCH_SIDE
    for r in range(NB):
        stream[r] = tn(patches, near_block(0, r)) + row_block(N_PATCH, r)
    for i in range(side):
        span = slice(i * side, (i + 1) * side)
        for r in range(2):
            stream[r, span, :] = stream[r, span, :] + spot_ref[r, i : i + 1, :]
            stream[2 + r, span, :] = stream[2 + r, span, :] + spot_ref[r]

    def modulate(source, scale, shift):
        def body(at):
            norm, _ = normed(wide(source, at))
            put(low_in, 0, at, norm * (1.0 + scale) + shift)

        over_rows(body)

    def transposed(base, ref, count):
        over(count, lambda r: acts_ref.__setitem__(base + r, ref[r].T))

    modulate(stream, mod(1), mod(0))
    transposed(L_ATT, low_in, NB)
    arrived(0)

    def qkv_step(c):
        total = nn(low_in[0], w_ref[AT_QKV + c])
        for r in range(1, NB):
            total += nn(low_in[r], w_ref[AT_QKV + r * QB + c])
        qkv[c] = (total + bias_ref[c]).astype(bf16)

    over(QB, qkv_step)

    def attend(c):
        for half in range(2):
            span = slice(half * 128, (half + 1) * 128)
            q, k, v = qkv[c, :, span], qkv[NB + c, :, span], qkv[2 * NB + c, :, span]
            parts = []
            for side in range(2):
                scores = nt(masked(q, side), k) * att_scale
                top = jnp.max(scores, axis=-1, keepdims=True)
                power = jnp.exp(scores - top)
                prob = power / jnp.sum(power, axis=-1, keepdims=True)
                probs[c * 4 + half * 2 + side] = prob
                parts.append(nn(prob.astype(bf16), v))
            low_att[c, :, span] = jnp.where(lower, parts[0], parts[1]).astype(bf16)

    over(NB, attend)
    transposed(L_OUT, low_att, NB)
    arrived(1)

    def out_step(c):
        total = nn(low_att[0], w_ref[AT_OUT + c])
        for r in range(1, NB):
            total += nn(low_att[r], w_ref[AT_OUT + r * NB + c])
        out_att[c] = total + bias_ref[B_OUT + c]

    over(NB, out_step)

    def mid_step(at):
        branch = mod(2) * wide(out_att, at)
        collect(S_SQ_ATT, branch * branch)
        value = wide(stream, at) + branch
        put(middle, 0, at, value)
        norm, _ = normed(value)
        put(low_in, 0, at, norm * (1.0 + mod(4)) + mod(3))

    over_rows(mid_step)
    transposed(L_MLP, low_in, NB)
    arrived(2)

    def up_step(c):
        total = nn(low_in[0], w_ref[AT_UP + c])
        for r in range(1, NB):
            total += nn(low_in[r], w_ref[AT_UP + r * HB + c])
        value, back = gelu_pair(total + bias_ref[B_UP + c])
        slope[c] = back
        low = value.astype(bf16)
        hid[c] = low
        acts_ref[L_HID + c] = low.T

    over(HB, up_step)
    arrived(3)

    def down_step(c):
        total = nn(hid[0], w_ref[AT_DOWN + c])
        for r in range(1, HB):
            total += nn(hid[r], w_ref[AT_DOWN + r * NB + c])
        out_mlp[c] = total + bias_ref[B_DOWN + c]

    over(NB, down_step)

    def end_step(at):
        branch = mod(5) * wide(out_mlp, at)
        collect(S_SQ_MLP, branch * branch)
        value = wide(middle, at) + branch
        collect(S_SQ_END, value * value)
        put(last, 0, at, value)
        norm, _ = normed(value)
        put(low_in, 0, at, norm * (1.0 + mod(7)) + mod(6))

    over_rows(end_step)
    predicted = nt(near_block(PATCH_DIM, 0), low_in[0])
    for r in range(1, NB):
        predicted += nt(near_block(PATCH_DIM, r), low_in[r])
    mismatch = predicted - noise_ref[...]
    loss_sum = jnp.sum(mismatch * mismatch)
    pred_low = (loss_factor * mismatch).astype(bf16)
    def put_rows(row, count, r, value):
        for i in range(2):
            ends_ref[2 * r + i, row : row + count, :] = value[:, i * 128 : (i + 1) * 128]

    for r in range(NB):
        put_rows(PATCH_DIM, PATCH_DIM, r, nn(pred_low, low_in[r]))
        flow[r] = tn(pred_low, near_block(PATCH_DIM, r))

    def end_back(at):
        grad = wide(flow, at)
        norm, value = norm_back(grad, wide(last, at), mod(7))
        collect(S_DSC_F, grad * norm)
        collect(S_DSH_F, grad)
        put(last, 0, at, value)
        collect(S_DG_M, value * wide(out_mlp, at))
        down = value * mod(5)
        collect(S_DOWN, down)
        put(acts_ref, R_DOWN, at, down)

    over_rows(end_back)

    def up_back(c):
        total = nt(acts_ref[R_DOWN], w_ref[AT_DOWN + c * NB])
        for j in range(1, NB):
            total += nt(acts_ref[R_DOWN + j], w_ref[AT_DOWN + c * NB + j])
        value = total * slope[c]
        dbias_ref[2 * NB + c] = jnp.sum(value, axis=0, keepdims=True)
        acts_ref[R_UP + c] = value.astype(bf16)

    over(HB, up_back)

    def mlp_back(r):
        total = nt(acts_ref[R_UP], w_ref[AT_UP + r * HB])
        for c in range(1, HB):
            total += nt(acts_ref[R_UP + c], w_ref[AT_UP + r * HB + c])
        flow[r] = total

    over(NB, mlp_back)

    def mid_back(at):
        grad = wide(flow, at)
        norm, value = norm_back(grad, wide(middle, at), mod(4))
        collect(S_DSC_M, grad * norm)
        collect(S_DSH_M, grad)
        value = value + wide(last, at)
        put(middle, 0, at, value)
        collect(S_DG_A, value * wide(out_att, at))
        proj = value * mod(2)
        collect(S_OUT, proj)
        put(acts_ref, R_OUT, at, proj)

    over_rows(mid_back)

    def att_back(r):
        total = nt(acts_ref[R_OUT], w_ref[AT_OUT + r * NB])
        for c in range(1, NB):
            total += nt(acts_ref[R_OUT + c], w_ref[AT_OUT + r * NB + c])
        low_att[r] = total.astype(bf16)

    over(NB, att_back)

    def attend_back(c):
        for half in range(2):
            span = slice(half * 128, (half + 1) * 128)
            q, k, v = qkv[c, :, span], qkv[NB + c, :, span], qkv[2 * NB + c, :, span]
            grad = low_att[c, :, span]
            found = []
            for side in range(2):
                prob = probs[c * 4 + half * 2 + side]
                dprob = nt(masked(grad, side), v)
                dvalue = tn(prob.astype(bf16), grad)
                dscore = prob * (dprob - jnp.sum(dprob * prob, axis=-1, keepdims=True))
                low = dscore.astype(bf16)
                found.append((nn(low, k) * att_scale, tn(low, q) * att_scale, dvalue))
            merged = [jnp.where(lower, one, two) for one, two in zip(*found)]
            for i in range(3):
                acts_ref[R_QKV + i * NB + c, :, span] = merged[i].astype(bf16)
            dbias_ref[c, :, span] = jnp.sum(merged[0], axis=0, keepdims=True)
            dbias_ref[NB + c, :, span] = jnp.sum(merged[2], axis=0, keepdims=True)

    over(NB, attend_back)

    def in_back(r):
        total = nt(acts_ref[R_QKV], w_ref[AT_QKV + r * QB])
        for c in range(1, QB):
            total += nt(acts_ref[R_QKV + c], w_ref[AT_QKV + r * QB + c])
        flow[r] = total

    over(NB, in_back)

    def first_back(at):
        grad = wide(flow, at)
        norm, value = norm_back(grad, wide(stream, at), mod(1))
        collect(S_DSC_A, grad * norm)
        collect(S_DSH_A, grad)
        value = value + wide(middle, at)
        collect(S_PATCH, value)
        put(low_in, 0, at, value)

    over_rows(first_back)
    for r in range(NB):
        put_rows(0, PATCH_DIM, r, nn(patches, low_in[r]))

    def total_of(which):
        return jnp.sum(sums[which], axis=0, keepdims=True)

    for i in range(8):
        value = total_of(S_DSH_A + i)
        for o in range(LANES):
            dmod_ref[i * LANES + o : i * LANES + o + 1, :] = value[:, o * 128 : (o + 1) * 128]
    for row, which in ((T_PATCH, S_PATCH), (T_OUT, S_OUT), (T_DOWN, S_DOWN)):
        value = total_of(which)
        for r in range(NB):
            put_rows(row, 1, r, value[:, r * BLK : (r + 1) * BLK])
    for r in range(NB):
        put_rows(T_QUERY, 1, r, dbias_ref[r])
        put_rows(T_VALUE, 1, r, dbias_ref[NB + r])
        for i in range(FF // D):
            put_rows(T_UP + i, 1, r, dbias_ref[2 * NB + i * NB + r])
    ends_ref[:, T_END:, :] = jnp.zeros((LANES, TOKEN_ROWS - T_END, 128), f32)
    row = lax.broadcasted_iota(jnp.int32, (8, 128), 0)
    found = jnp.where(row == 0, loss_sum, 0.0)
    for i in range(3):
        found = jnp.where(row == i + 1, jnp.sum(sums[i]), found)
    stats_ref[...] = found


def block_step(place, tiles, patches, noise, spots, near, mods, loss_factor):
    vmem = pl.BlockSpec(memory_space=pltpu.VMEM)
    macs = 3 * SEQ * BIG * BLK * BLK
    return pl.pallas_call(
        functools.partial(block_body, loss_factor),
        out_shape=[
            jax.ShapeDtypeStruct((ACTS, BLK, BLK), bf16),
            jax.ShapeDtypeStruct((8 * LANES, 128), f32),
            jax.ShapeDtypeStruct((LANES, TOKEN_ROWS, 128), f32),
            jax.ShapeDtypeStruct((8, 128), f32),
        ],
        in_specs=[pl.BlockSpec(memory_space=pltpu.SMEM), pl.BlockSpec(memory_space=pl.ANY)] + [vmem] * 5,
        out_specs=[vmem] * 4,
        scratch_shapes=[
            pltpu.VMEM((BIG, BLK, BLK), bf16),
            pltpu.VMEM((NB, SEQ, BLK), f32),
            pltpu.VMEM((NB, SEQ, BLK), f32),
            pltpu.VMEM((NB, SEQ, BLK), f32),
            pltpu.VMEM((NB, SEQ, BLK), f32),
            pltpu.VMEM((NB, SEQ, BLK), f32),
            pltpu.VMEM((NB, SEQ, BLK), bf16),
            pltpu.VMEM((NB, SEQ, BLK), bf16),
            pltpu.VMEM((QB, SEQ, BLK), bf16),
            pltpu.VMEM((HB, SEQ, BLK), bf16),
            pltpu.VMEM((HB, SEQ, BLK), f32),
            pltpu.VMEM((HEADS, SEQ, SEQ), f32),
            pltpu.VMEM((NB, SEQ, BLK), f32),
            pltpu.VMEM((14, 8, D), f32),
            pltpu.VMEM((LANES, NEAR, 128), f32),
            pltpu.VMEM((B_DOWN + NB, 1, BLK), f32),
            pltpu.VMEM((8, D), f32),
            pltpu.VMEM((2 * NB + HB, 1, BLK), f32),
            pltpu.SemaphoreType.DMA((4,)),
        ],
        compiler_params=pltpu.CompilerParams(vmem_limit_bytes=54 << 20),
        cost_estimate=pl.CostEstimate(flops=2 * macs, bytes_accessed=BIG * BLK * BLK * 4, transcendentals=0),
        name="block_step",
    )(place, tiles, patches, noise, spots, near, mods)


def ada_front_body(row_ref, col_ref, cond_ref, tile_ref, out_ref):
    s = pl.program_id(0)

    @pl.when(s == 0)
    def _():
        out_ref[...] = jnp.zeros_like(out_ref)

    @pl.when(col_ref[s] >= 0)
    def _():
        c = col_ref[s]
        out_ref[c] = out_ref[c] + nn(cond_ref[row_ref[s]], tile_ref[0].astype(bf16))


def ada_front(row_of, col_of, cond_blocks, tile_master):
    per, images = tile_master.shape[0], cond_blocks.shape[1]
    return pl.pallas_call(
        ada_front_body,
        grid_spec=pltpu.PrefetchScalarGridSpec(
            num_scalar_prefetch=2,
            grid=(per,),
            in_specs=[
                pl.BlockSpec(cond_blocks.shape, lambda s, r, c: (0, 0, 0)),
                pl.BlockSpec((1, BLK, BLK), lambda s, r, c: (s, 0, 0)),
            ],
            out_specs=pl.BlockSpec((6 * NB, images, BLK), lambda s, r, c: (0, 0, 0)),
        ),
        out_shape=jax.ShapeDtypeStruct((6 * NB, images, BLK), f32),
        name="ada_front",
    )(row_of, col_of, cond_blocks, tile_master)


def ada_back_body(row_ref, col_ref, dmod_ref, tile_ref, out_ref):
    s = pl.program_id(0)

    @pl.when(s == 0)
    def _():
        out_ref[...] = jnp.zeros_like(out_ref)

    @pl.when(col_ref[s] >= 0)
    def _():
        r = row_ref[s]
        out_ref[r] = out_ref[r] + nt(dmod_ref[col_ref[s]], tile_ref[0].astype(bf16))


def ada_back(row_of, col_of, dmod_blocks, tile_master):
    per, images = tile_master.shape[0], dmod_blocks.shape[1]
    return pl.pallas_call(
        ada_back_body,
        grid_spec=pltpu.PrefetchScalarGridSpec(
            num_scalar_prefetch=2,
            grid=(per,),
            in_specs=[
                pl.BlockSpec(dmod_blocks.shape, lambda s, r, c: (0, 0, 0)),
                pl.BlockSpec((1, BLK, BLK), lambda s, r, c: (s, 0, 0)),
            ],
            out_specs=pl.BlockSpec((NB, images, BLK), lambda s, r, c: (0, 0, 0)),
        ),
        out_shape=jax.ShapeDtypeStruct((NB, images, BLK), f32),
        name="ada_back",
    )(row_of, col_of, dmod_blocks, tile_master)


def tile_grad_body(left_ref, right_ref, acts_ref, out_ref):
    s = pl.program_id(0)
    out_ref[0] = nn(acts_ref[left_ref[s]], acts_ref[right_ref[s]]).astype(bf16)


def tile_grads(left_of, right_of, acts):
    count = left_of.shape[0]
    return pl.pallas_call(
        tile_grad_body,
        grid_spec=pltpu.PrefetchScalarGridSpec(
            num_scalar_prefetch=2,
            grid=(count,),
            in_specs=[pl.BlockSpec(acts.shape, lambda s, a, b: (0, 0, 0))],
            out_specs=pl.BlockSpec((1, BLK, BLK), lambda s, a, b: (s, 0, 0)),
        ),
        out_shape=jax.ShapeDtypeStruct((count, BLK, BLK), bf16),
        compiler_params=pltpu.CompilerParams(vmem_limit_bytes=40 << 20),
        name="tile_grads",
    )(left_of, right_of, acts)


def adam_body(
    group, factors, where_ref, row_ref, col_ref,
    norm_ref, totals_ref, grads_ref, cond_ref, dmod_ref, bases_ref, moment_ref, second_ref, row_grad_ref, row_master_ref, row_moment_ref, row_second_ref,
    new_moment_ref, new_second_ref, update_ref, new_row_moment_ref, new_row_second_ref, row_update_ref,
    loss_ref, grad_norm_ref, act_rms_ref,
):
    step = pl.program_id(0)

    @pl.when(step == 0)
    def _():
        loss_ref[0] = totals_ref[0, 0] * factors[0]
        grad_norm_ref[0] = jnp.sqrt(norm_ref[...])[0, 0]
        roots = jnp.sqrt(totals_ref[...] * factors[1])
        for i in range(3):
            act_rms_ref[i] = roots[i + 1, 0]

    factor = clip_at / jnp.maximum(jnp.sqrt(norm_ref[0:1, 0:1]), clip_at)

    def moved(moment, second, grad):
        new_moment = beta_one * moment + (1.0 - beta_one) * grad
        new_second = beta_two * second + (1.0 - beta_two) * grad * grad
        return new_moment, new_second, new_moment / (jnp.sqrt(new_second) + adam_eps)

    for j in range(group):
        s = step * group + j
        r, c = row_ref[s], col_ref[s]
        cond = jnp.concatenate([cond_ref[2 * r], cond_ref[2 * r + 1]], axis=1)
        thin = tn(cond, dmod_ref[jnp.maximum(c, 0)]).astype(bf16)
        grad = jnp.where(c >= 0, thin, grads_ref[where_ref[s]])
        left, right = bases_ref[j, 0].astype(bf16), bases_ref[j, 1].astype(bf16)
        turned = factor * tn(left, nn(grad, right).astype(bf16))
        moment, second, direction = moved(moment_ref[j], second_ref[j], turned)
        new_moment_ref[j] = moment
        new_second_ref[j] = second
        update_ref[j] = -rate_step * nt(nn(left, direction.astype(bf16)).astype(bf16), right)

    moment, second, direction = moved(row_moment_ref[...], row_second_ref[...], factor * row_grad_ref[...])
    new_row_moment_ref[...] = moment
    new_row_second_ref[...] = second
    row_update_ref[...] = -rate_step * (direction + decay_rate * row_master_ref[...])


def adam(factors, where, row_of, col_of, norm, totals, grads, conds, dmod_blocks, bases, moment, second, row_grad, row_master, row_moment, row_second):
    per = moment.shape[0]
    group = next(g for g in (ADAM_GROUP, 3, 2, 1) if per % g == 0)
    steps = per // group
    tile = pl.BlockSpec((group, BLK, BLK), lambda s, *_: (s, 0, 0))
    row_count, columns = row_master.shape
    row = pl.BlockSpec((-(-row_count // (8 * steps)) * 8, columns), lambda s, *_: (s, 0))

    def whole(array):
        return pl.BlockSpec(array.shape, lambda s, *_: (0,) * array.ndim)

    shape = jax.ShapeDtypeStruct(moment.shape, f32)
    row_shape = jax.ShapeDtypeStruct(row_master.shape, f32)
    return pl.pallas_call(
        functools.partial(adam_body, group, factors),
        grid_spec=pltpu.PrefetchScalarGridSpec(
            num_scalar_prefetch=3,
            grid=(steps,),
            in_specs=[
                whole(norm),
                whole(totals),
                whole(grads),
                whole(conds),
                whole(dmod_blocks),
                pl.BlockSpec((group, 2, BLK, BLK), lambda s, *_: (s, 0, 0, 0)),
                tile,
                tile,
                row,
                row,
                row,
                row,
            ],
            out_specs=[tile] * 3 + [row] * 3 + [pl.BlockSpec(memory_space=pltpu.SMEM)] * 3,
        ),
        out_shape=[shape] * 3 + [row_shape] * 3 + [jax.ShapeDtypeStruct((n,), f32) for n in (1, 1, 3)],
        compiler_params=pltpu.CompilerParams(vmem_limit_bytes=61 << 20),
        name="adam",
    )(where, row_of, col_of, norm, totals, grads, conds, dmod_blocks, bases, moment, second, row_grad, row_master, row_moment, row_second)


def spread_body(
    cap, n_third,
    slot_ref, row_ref, col_ref, step_ref, name_ref, tiles_ref, rows_ref,
    out_ref, near_ref, mods_ref, freq_ref, label_ref, time_ref, cond_ref, pre_ref, own_cond_ref,
    tile, pack, ids, near, times, conds, near_wide, cond_group, product, part, part_out, part_in,
    load_sem, keep_sem, send_sem, recv_sem, small_send, small_recv,
):
    z, s = lax.axis_index("grp"), lax.axis_index("shard")
    per = tile.shape[0]
    images = GROUPS * SHARDS
    third = cap // 3
    both = cap - 2 * third
    x_at, y_at, c_at, z_at = (z, s ^ 2), (z, s ^ 4), (z, s ^ 1), (z ^ 1, s)
    far_z = [(lax.rem(z + i, GROUPS), s) for i in range(1, GROUPS)]
    near_s = [(z, s ^ i) for i in range(1, SHARDS)]

    barrier = pltpu.get_barrier_semaphore()
    for peer in far_z + near_s:
        pl.semaphore_signal(barrier, inc=1, device_id=peer, device_id_type=MESH_ID)
    load = pltpu.make_async_copy(tiles_ref, tile, load_sem)
    load.start()

    def block_rows(index, count):
        return pl.ds(pl.multiple_of(index * count, count), count)

    lane = lax.broadcasted_iota(jnp.int32, (8, 128), 1).astype(f32)
    angle = step_ref[0].astype(f32) * jnp.exp(-math.log(10000.0) * lane / (FREQ // 2))
    line = lax.broadcasted_iota(jnp.int32, (8, 128), 0)
    known = jnp.where(line == 0, jnp.cos(angle), jnp.where(line == 1, jnp.sin(angle), name_ref[0].astype(f32)))
    ids[block_rows(s * GROUPS + z, 8), :] = known
    near_wide[...] = jnp.zeros_like(near_wide)
    near_wide[: NEAR_REAL - 3, :] = rows_ref[NEAR_START : NEAR_START + NEAR_REAL - 3, :]
    near_wide[NEAR_REAL - 3 : NEAR_REAL, :] = rows_ref[NEAR_START + NEAR_REAL - 3 : NEAR_START + NEAR_REAL, :]
    near[s] = near_wide[...].astype(bf16)
    near_wide[...] = near_wide[...].astype(bf16).astype(f32)
    pl.semaphore_wait(barrier, len(far_z) + len(near_s))

    sent = []

    def push(src, dst, peer, index):
        copy = pltpu.make_async_remote_copy(
            src_ref=src, dst_ref=dst, send_sem=small_send.at[index], recv_sem=small_recv.at[index],
            device_id=peer, device_id_type=MESH_ID,
        )
        copy.start()
        sent.append(copy)
        return copy

    def to_group(stage, pairs):
        first = len(far_z) + stage * len(near_s)
        return [push(*pairs(peer[1]), peer, first + i) for i, peer in enumerate(near_s)]

    def got(copies):
        for copy in copies:
            copy.wait_recv()

    own_ids = ids.at[block_rows(s * GROUPS + z, 8)]
    id_far = [push(own_ids, own_ids, peer, i) for i, peer in enumerate(far_z)]
    near_copies = to_group(0, lambda p: (near.at[s], near.at[s]))

    parity = lax.rem(z, 2)
    starts = (both + parity * third, 0, both + third - parity * third)

    def chunk_of(index):
        kind, at = divmod(index, n_third)
        size = both if kind == 1 else third
        first, last = at * size // n_third, (at + 1) * size // n_third
        return starts[kind] + first, last - first

    def chunk(index):
        return pl.ds(*chunk_of(index))

    load.wait()
    big = []

    def send(kind, stream, index, peer, src, owner, arrives):
        copy = pltpu.make_async_remote_copy(
            src_ref=src, dst_ref=out_ref.at[owner, chunk(index)],
            send_sem=send_sem.at[kind, index], recv_sem=recv_sem.at[stream, arrives],
            device_id=peer, device_id_type=MESH_ID,
        )
        copy.start()
        big.append(copy)

    def wait_for(stream, index, owner):
        place = out_ref.at[owner, chunk(index)]
        pltpu.make_async_remote_copy(
            src_ref=place, dst_ref=place, send_sem=send_sem.at[0, index], recv_sem=recv_sem.at[stream, index],
            device_id=x_at, device_id_type=MESH_ID,
        ).wait_recv()

    def pack_chunk(index):
        start, count = chunk_of(index)

        def one(i, unused):
            p = start + i
            pack[p] = tile[slot_ref[p]].astype(bf16)
            return unused

        lax.fori_loop(0, count, one, 0)

    def send_mine(index):
        src = pack.at[chunk(index)]
        if index < 2 * n_third:
            send(0, 0, index, x_at, src, s, index)
            send(1, 1, index, y_at, src, s, index)
        send(2, 3, index, c_at, src, s, index)

    owners = (s ^ 2, s ^ 4, s ^ 6)

    def pass_on(which, index):
        owner = owners[which]
        wait_for(which, index, owner)
        here = out_ref.at[owner, chunk(index)]
        if index < 2 * n_third:
            if which == 0 and index % 2 == 0:
                send(6, 2, index, y_at, here, owner, index)
            if which == 1 and index % 2 == 1:
                send(7, 2, index, x_at, here, owner, index)
        if index < n_third:
            send(8 + which, which, index, z_at, here, owner, 2 * n_third + index)
        send(3 + which, 4 + which, index, c_at, here, owner, index)

    for j in range(n_third):
        pack_chunk(j)
        send_mine(j)
    got(id_far)
    span = block_rows(s, 8 * GROUPS)
    id_near = to_group(1, lambda p: (ids.at[span], ids.at[span]))
    for j in range(n_third, 3 * n_third):
        pack_chunk(j)
    keep = pltpu.make_async_copy(pack, out_ref.at[s, pl.ds(0, cap)], keep_sem)
    keep.start()
    stages = {}

    def silu_low(value):
        return (value * jax.nn.sigmoid(value)).astype(bf16)

    def row_slice(start, count):
        return rows_ref[start : start + count, :].astype(bf16)

    def time_stage():
        got(id_near)
        freq = jnp.concatenate([ids[pl.ds(i, images, stride=8), :] for i in range(2)], axis=1).astype(bf16)
        freq_ref[...] = freq
        label_ref[...] = ids[pl.ds(2, images, stride=8), :]
        pre = nn(freq, row_slice(NCLASS, FREQ)) + near_wide[N_TIME1 : N_TIME1 + 1, :]
        pre_ref[...] = pre
        times[s] = silu_low(pre)
        stages["time"] = to_group(2, lambda p: (times.at[s], times.at[s]))

    def cond_stage():
        got(stages["time"])
        total = jnp.zeros((images, 128), f32) + near_wide[N_TIME2 : N_TIME2 + 1, :]
        for o in range(SHARDS):
            total += nn(times[o], row_slice(NCLASS + FREQ + o * 128, 128))
        hot = label_ref[...].astype(jnp.int32)[:, :1] == lax.broadcasted_iota(jnp.int32, (images, D), 1)
        total += nn(hot.astype(bf16), row_slice(0, D))
        own_cond_ref[...] = total
        conds[s] = silu_low(total)
        stages["cond"] = to_group(3, lambda p: (conds.at[s], conds.at[s]))

    def group_stage():
        got(stages["cond"])
        at = lax.broadcasted_iota(jnp.int32, (SHARDS, images), 1)
        row = lax.broadcasted_iota(jnp.int32, (SHARDS, images), 0)
        pick = (at == row * GROUPS + z).astype(bf16)
        for o in range(SHARDS):
            half = o % 2
            cond_group[o // 2, :, half * 128 : (half + 1) * 128] = nn(pick, conds[o])

    def ada_stage(start, count):
        for j in range(start, start + count):
            product[j] = nn(cond_group[row_ref[j]].astype(bf16), tile[j].astype(bf16))

    def part_stage():
        part[...] = jnp.zeros_like(part)

        def column(c, unused):
            total = jnp.zeros((SHARDS, BLK), f32)
            for j in range(per):
                total += jnp.where(col_ref[j] == c, 1.0, 0.0) * product[j]
            for half in range(2):
                part[block_rows(2 * c + half, 8), :] = total[:, half * 128 : (half + 1) * 128]
            return unused

        lax.fori_loop(0, 6 * NB, column, 0)
        for i in range(6):
            place = block_rows(i * LANES + s, 8)
            part[place, :] = part[place, :] + near_wide[N_ADA + i : N_ADA + i + 1, :]
        for i in range(2):
            total = jnp.zeros((SHARDS, 128), f32) + near_wide[N_FINAL + i : N_FINAL + i + 1, :]
            for r in range(NB):
                weight = row_slice(NCLASS + FREQ + D + i * D + r * BLK, BLK)
                total += nn(cond_group[r].astype(bf16), weight)
            part[block_rows((6 + i) * LANES + s, 8), :] = total
        for o in range(SHARDS):
            part_out[o] = part[pl.ds(o, 8 * LANES, stride=8), :]
        part_in[s] = part_out[s]
        stages["part"] = to_group(4, lambda p: (part_out.at[p], part_in.at[s]))

    def mod_stage():
        got(stages["part"])
        total = part_in[0]
        for o in range(1, SHARDS):
            total += part_in[o]
        mods_ref[...] = total
        got(near_copies)
        near_ref[...] = near[...]
        time_ref[...] = times[...]
        cond_ref[...] = conds[...]

    cut = per // 3
    hooks = [
        (0.10, time_stage), (0.30, cond_stage), (0.50, group_stage), (0.55, lambda: ada_stage(0, cut)),
        (0.60, lambda: ada_stage(cut, cut)), (0.65, lambda: ada_stage(2 * cut, per - 2 * cut)), (0.70, part_stage), (2.0, mod_stage),
    ]
    seen = [0]
    steps = [0]

    def hook(last=False):
        steps[0] += 1
        while hooks and (last or steps[0] >= hooks[0][0] * 3 * n_third):
            hooks.pop(0)[1]()

    def z_next():
        order = [(w, 2 * n_third + j) for j in range(n_third) for w in (0, 1)]
        order += [(2, 2 * n_third + j) for j in range(n_third)]
        if seen[0] < len(order):
            pass_on(*order[seen[0]])
            seen[0] += 1

    for j in range(n_third):
        pass_on(0, j)
        pass_on(1, j)
        hook()
        if j:
            z_next()
    for j in range(n_third, 3 * n_third):
        send_mine(j)
    for j in range(n_third):
        pass_on(2, j)
        if j % 2:
            z_next()
            hook()
    for j in range(n_third, 2 * n_third):
        pass_on(0, j)
        pass_on(1, j)
        hook()
        z_next()
    for j in range(n_third, 2 * n_third):
        pass_on(2, j)
        if j % 2:
            z_next()
            hook()
    while seen[0] < 3 * n_third:
        z_next()
    hook(last=True)
    for index in range(3 * n_third):
        wait_for(3, index, s ^ 1)
        for which in range(3):
            wait_for(4 + which, index, owners[which] ^ 1)
    keep.wait()
    for copy in big + sent:
        copy.wait_send()


def spread(cap, slot_of, row_of, col_of, timesteps, labels, tile_master, row_master):
    per = tile_master.shape[0]
    n_third = 5
    images = GROUPS * SHARDS
    vmem = pl.BlockSpec(memory_space=pltpu.VMEM)
    smem = pl.BlockSpec(memory_space=pltpu.SMEM)
    anywhere = pl.BlockSpec(memory_space=pl.ANY)
    small = (GROUPS - 1) + 5 * (SHARDS - 1)
    return pl.pallas_call(
        functools.partial(spread_body, cap, n_third),
        out_shape=[
            jax.ShapeDtypeStruct((SHARDS, per, BLK, BLK), bf16),
            jax.ShapeDtypeStruct((LANES, NEAR, 128), bf16),
            jax.ShapeDtypeStruct((8 * LANES, 128), f32),
            jax.ShapeDtypeStruct((images, FREQ), bf16),
            jax.ShapeDtypeStruct((images, 128), f32),
            jax.ShapeDtypeStruct((SHARDS, images, 128), bf16),
            jax.ShapeDtypeStruct((SHARDS, images, 128), bf16),
            jax.ShapeDtypeStruct((images, 128), f32),
            jax.ShapeDtypeStruct((images, 128), f32),
        ],
        in_specs=[smem] * 5 + [anywhere, vmem],
        out_specs=[anywhere] + [vmem] * 8,
        scratch_shapes=[
            pltpu.VMEM((per, BLK, BLK), f32),
            pltpu.VMEM((cap, BLK, BLK), bf16),
            pltpu.VMEM((images * 8, 128), f32),
            pltpu.VMEM((LANES, NEAR, 128), bf16),
            pltpu.VMEM((SHARDS, images, 128), bf16),
            pltpu.VMEM((SHARDS, images, 128), bf16),
            pltpu.VMEM((NEAR, 128), f32),
            pltpu.VMEM((NB, SHARDS, BLK), f32),
            pltpu.VMEM((per, SHARDS, BLK), f32),
            pltpu.VMEM((8 * LANES * 8, 128), f32),
            pltpu.VMEM((SHARDS, 8 * LANES, 128), f32),
            pltpu.VMEM((SHARDS, 8 * LANES, 128), f32),
            pltpu.SemaphoreType.DMA,
            pltpu.SemaphoreType.DMA,
            pltpu.SemaphoreType.DMA((11, 3 * n_third)),
            pltpu.SemaphoreType.DMA((7, 3 * n_third)),
            pltpu.SemaphoreType.DMA((small,)),
            pltpu.SemaphoreType.DMA((small,)),
        ],
        compiler_params=pltpu.CompilerParams(collective_id=cap, has_side_effects=True, vmem_limit_bytes=61 << 20),
        name="spread",
    )(slot_of, row_of, col_of, timesteps, labels, tile_master, row_master)

RING = 6
SUM_LAG = 2
Z_STEP = 1
Z_LAG = SUM_LAG + 4 * Z_STEP
ADA_PARTS = 6


def collect_body(
    cap, ch,
    left_ref, right_ref, row_ref, col_ref, count_ref,
    acts_ref, dmod_ref, ends_ref, stats_ref, time_ref, cond_ref, freq_ref, label_ref, pre_ref, own_cond_ref, rows_ref, tiles_ref,
    grads_ref, d_blocks_ref, own_rows_ref, norm_ref, stat_ref,
    out_c, in_c, out_d, out_x, out_y, in_dx, in_dy, in_x, in_y, total, low_in, high_in, final,
    tile, product, all_d, wide_d, all_stats, tok_out, tok_in, tok_z, tokens, part_out, part_in, pre_out, pre_in, own_dcond, own_dpre,
    vectors, squares, square_in,
    c_send, c_recv, d_send, dx_recv, dy_recv, x_send, x_recv, y_send, y_recv, up_send, low_recv, high_recv, final_recv, down_send,
    keep_sem, load_sem, small_send, small_recv,
):
    z, s = lax.axis_index("grp"), lax.axis_index("shard")
    per = product.shape[0]
    images = GROUPS * SHARDS
    chunks = cap // ch
    x_at, y_at, c_at = (z, s ^ 2), (z, s ^ 4), (z, s ^ 1)
    far_z = [(lax.rem(z + i, GROUPS), s) for i in range(1, GROUPS)]
    near_s = [(z, s ^ i) for i in range(1, SHARDS)]
    half = BLK // 2
    upper, lower = pl.ds(0, half), pl.ds(half, half)

    barrier = pltpu.get_barrier_semaphore()
    for peer in far_z + near_s:
        pl.semaphore_signal(barrier, inc=1, device_id=peer, device_id_type=MESH_ID)

    def remote(src, dst, sent, received, peer):
        return pltpu.make_async_remote_copy(
            src_ref=src, dst_ref=dst, send_sem=sent, recv_sem=received, device_id=peer, device_id_type=MESH_ID
        )

    def block_rows(index, count):
        return pl.ds(pl.multiple_of(index * count, count), count)

    def far(stage, src, dst):
        return [
            remote(src, dst, small_send.at[stage * 3 + i], small_recv.at[stage * 3 + i], peer) for i, peer in enumerate(far_z)
        ]

    def group(stage, src_of, dst):
        first = 9 + stage * 7
        return [
            remote(src_of(peer[1]), dst, small_send.at[first + i], small_recv.at[first + i], peer)
            for i, peer in enumerate(near_s)
        ]

    def direct(stage, ref):
        first = 9 + stage * 7
        return [
            remote(ref, ref, small_send.at[first + i], small_recv.at[first + i], peer)
            for i, peer in enumerate((x_at, y_at, (z, s ^ 6), c_at))
        ]

    def passed(stage, ref_of):
        first = 9 + stage * 7 + 4
        return [
            remote(ref_of(o), ref_of(o), small_send.at[first + i], small_recv.at[first + i], c_at)
            for i, o in enumerate((s ^ 2, s ^ 4, s ^ 6))
        ]

    own_d = all_d.at[block_rows(s * GROUPS + z, 8 * LANES)]
    own_stat = all_stats.at[block_rows(s * GROUPS + z, 8)]
    group_d = all_d.at[block_rows(s, 8 * LANES * GROUPS)]
    group_stat = all_stats.at[block_rows(s, 8 * GROUPS)]

    def small_copies(name):
        if name == "d_far":
            return far(0, own_d, own_d)
        if name == "stat_far":
            return far(1, own_stat, own_stat)
        if name == "tok_far":
            return far(2, tok_z.at[z], tok_z.at[z])
        if name == "tok":
            return group(0, lambda p: tok_out.at[p], tok_in.at[s])
        if name == "d":
            return direct(1, group_d)
        if name == "stat":
            return direct(2, group_stat)
        if name == "d_more":
            return passed(1, lambda o: all_d.at[block_rows(o, 8 * LANES * GROUPS)])
        if name == "stat_more":
            return passed(2, lambda o: all_stats.at[block_rows(o, 8 * GROUPS)])
        if name == "part":
            return group(3, lambda p: part_out.at[p], part_in.at[s])
        if name == "pre":
            return group(4, lambda p: pre_out.at[p], pre_in.at[s])
        return group(5, lambda p: square_in.at[s], square_in.at[s])

    def begin(*names):
        for name in names:
            for copy in small_copies(name):
                copy.start()

    def got(*names):
        for name in names:
            for copy in small_copies(name):
                copy.wait_recv()

    def load(part):
        count = tile.shape[0]
        return pltpu.make_async_copy(tiles_ref.at[pl.ds(part * count, count)], tile, load_sem)

    load(0).start()
    own_d[...] = dmod_ref[...].astype(bf16)
    own_stat[...] = stats_ref[...]
    tok_out[...] = ends_ref[...].astype(bf16)
    tok_in[s] = tok_out[s]
    squares[...] = jnp.zeros_like(squares)
    pl.semaphore_wait(barrier, len(far_z) + len(near_s))
    begin("d_far", "stat_far", "tok")

    def spread_stage():
        got("d_far", "stat_far")
        begin("d", "stat")
        got("tok")
        value = tok_in[0].astype(f32)
        for o in range(1, SHARDS):
            value += tok_in[o].astype(f32)
        tok_z[z] = value
        begin("tok_far")

    def pass_stage():
        got("d", "stat")
        begin("d_more", "stat_more")

    def order_stage():
        got("d_more", "stat_more", "tok_far")
        value = tok_z[0]
        for i in range(1, GROUPS):
            value += tok_z[i]
        tokens[...] = value
        value = all_stats[pl.ds(0, 8), :]
        for i in range(1, images):
            value += all_stats[pl.ds(8 * i, 8), :]
        stat_ref[...] = value

        def widen(i, unused):
            place = block_rows(i, 8 * LANES)
            wide_d[place, :] = all_d[place, :].astype(f32)
            return unused

        lax.fori_loop(0, images, widen, 0)
        for q in range(6 * LANES):
            d_blocks_ref[q // 2, :, (q % 2) * 128 : (q % 2 + 1) * 128] = wide_d[
                pl.ds(q, images, stride=8 * LANES), :
            ].astype(bf16)

    def own_columns(i):
        return wide_d[pl.ds(i * LANES + s, images, stride=8 * LANES), :]

    def ada_stage(part):
        count = tile.shape[0]
        load(part).wait()

        for j in range(count):
            at = part * count + j
            product[at] = nt(d_blocks_ref[jnp.maximum(col_ref[at], 0)], tile[j].astype(bf16))
        if (part + 1) * count < per:
            load(part + 1).start()

    def row_slice(start, count):
        return rows_ref[start : start + count, :].astype(bf16)

    final_at = NCLASS + FREQ + D

    def part_stage():
        def add(j, values):
            chosen = [jnp.logical_and(col_ref[j] >= 0, row_ref[j] == r) for r in range(NB)]
            return tuple(value + jnp.where(one, 1.0, 0.0) * product[j] for one, value in zip(chosen, values))

        values = []
        for r in range(NB):
            value = jnp.zeros((images, BLK), f32)
            for i in range(2):
                value += nt(own_columns(6 + i).astype(bf16), row_slice(final_at + i * D + r * BLK, BLK))
            values.append(value)
        values = lax.fori_loop(0, per, add, tuple(values))
        for r in range(NB):
            for i in range(2):
                part_out[2 * r + i] = values[r][:, i * 128 : (i + 1) * 128].astype(bf16)
        part_in[s] = part_out[s]
        begin("part")

    def slope(value):
        gate = jax.nn.sigmoid(value)
        return gate * (1.0 + value * (1.0 - gate))

    def cond_stage():
        got("part")
        value = part_in[0].astype(f32)
        for o in range(1, SHARDS):
            value += part_in[o].astype(f32)
        value = value * slope(own_cond_ref[...])
        own_dcond[...] = value
        for o in range(SHARDS):
            pre_out[o] = nt(value.astype(bf16), row_slice(NCLASS + FREQ + o * 128, 128)).astype(bf16)
        pre_in[s] = pre_out[s]
        begin("pre")

    def row_stage():
        got("pre")
        value = pre_in[0].astype(f32)
        for o in range(1, SHARDS):
            value += pre_in[o].astype(f32)
        value = value * slope(pre_ref[...])
        own_dpre[...] = value
        dpre_low, dcond = value.astype(bf16), own_dcond[...]
        dcond_low = dcond.astype(bf16)
        gathered = []

        def keep(start, value):
            own_rows_ref[start : start + value.shape[0], :] = value
            gathered.append(fold(value * value))

        hot = label_ref[...].astype(jnp.int32)[:, :1] == lax.broadcasted_iota(jnp.int32, (images, NCLASS), 1)
        keep(
            0,
            lax.dot_general(
                hot.astype(f32), dcond, (((0,), (0,)), ((), ())), preferred_element_type=f32, precision=lax.Precision.HIGHEST
            ),
        )
        keep(NCLASS, tn(freq_ref[...], dpre_low))
        for o in range(SHARDS):
            keep(NCLASS + FREQ + o * 128, tn(time_ref[o], dcond_low))
            for i in range(2):
                keep(final_at + i * D + o * 128, tn(cond_ref[o], own_columns(6 + i).astype(bf16)))
        keep(NEAR_START, tokens[: 2 * PATCH_DIM, :])

        vectors[...] = jnp.zeros_like(vectors)

        def vector(row, value):
            vectors[row : row + 1, :] = value

        vector(0, tokens[T_PATCH : T_PATCH + 1, :])
        vector(1, jnp.sum(value, axis=0, keepdims=True))
        vector(2, jnp.sum(dcond, axis=0, keepdims=True))
        vector(3, tokens[T_QUERY : T_QUERY + 1, :])
        vector(4, tokens[T_VALUE : T_VALUE + 1, :])
        vector(5, tokens[T_OUT : T_OUT + 1, :])
        vector(6, tokens[T_DOWN : T_DOWN + 1, :])
        for i in range(8):
            vector(7 + i if i < 6 else 7 + i + FF // D, jnp.sum(own_columns(i), axis=0, keepdims=True))
        for i in range(FF // D):
            vector(13 + i, tokens[T_UP + i : T_UP + i + 1, :])
        start = NEAR_START + 2 * PATCH_DIM
        rest = own_rows_ref.shape[0] - start
        whole = rest // 8 * 8
        own_rows_ref[start : start + whole, :] = vectors[:whole, :]
        own_rows_ref[start + whole : start + rest, :] = vectors[whole:rest, :]
        value = fold(vectors[...] * vectors[...])
        for piece in gathered:
            value += piece
        squares[:, :128] = squares[:, :128] + value

    def slot_of(i):
        return lax.rem(i + 2 * RING, RING)

    def block(owner, p):
        at = owner * per + p
        return nn(acts_ref[left_ref[at]], acts_ref[right_ref[at]])

    targets = (s ^ 6, s ^ 2, s ^ 4, s)

    def c_copy(slot, item):
        return remote(out_c.at[slot, item], in_c.at[slot, item], c_send.at[slot, item], c_recv.at[slot, item], c_at)

    def dx_copy(slot):
        return remote(out_d.at[slot, :, upper], in_dx.at[slot], d_send.at[slot, 0], dx_recv.at[slot], x_at)

    def dy_copy(slot):
        return remote(out_d.at[slot, :, lower], in_dy.at[slot], d_send.at[slot, 1], dy_recv.at[slot], y_at)

    def x_copy(slot):
        return remote(out_x.at[slot], in_x.at[slot], x_send.at[slot], x_recv.at[slot], x_at)

    def y_copy(slot):
        return remote(out_y.at[slot], in_y.at[slot], y_send.at[slot], y_recv.at[slot], y_at)

    def inside(i):
        return jnp.logical_and(i >= 0, i < chunks)

    def each(body):
        if ch == 1:
            body(0)
            return

        def one(c, unused):
            body(c)
            return unused

        lax.fori_loop(0, ch, one, 0)

    def for_sibling(n):
        slot = slot_of(n)
        for items, at in (((0,), n + 1), ((1, 2, 3), n)):

            @pl.when(inside(at))
            def _():
                for item in items:
                    each(lambda c: out_c.__setitem__((slot, item, c), block(targets[item] ^ 1, at * ch + c).astype(bf16)))
                for item in items:
                    c_copy(slot, item).start()

    def for_owners(i):
        slot, before = slot_of(i), slot_of(i - 1)

        @pl.when(inside(i + 1))
        def _():
            c_copy(slot, 0).wait_recv()

            def one(c):
                value = block(targets[0], (i + 1) * ch + c) + in_c[slot, 0, c].astype(f32)
                out_d[slot, c] = value.astype(bf16)

            each(one)
            dx_copy(slot).start()
            dy_copy(slot).start()

        @pl.when(inside(i))
        def _():
            for item in (1, 2, 3):
                c_copy(slot, item).wait_recv()
            dy_copy(before).wait_recv()
            dx_copy(before).wait_recv()

            def one(c):
                value = block(targets[1], i * ch + c) + in_c[slot, 1, c].astype(f32)
                out_x[slot, c, upper] = value[:half].astype(bf16)
                out_x[slot, c, lower] = (value[half:] + in_dy[before, c].astype(f32)).astype(bf16)

            def two(c):
                value = block(targets[2], i * ch + c) + in_c[slot, 2, c].astype(f32)
                out_y[slot, c, upper] = (value[:half] + in_dx[before, c].astype(f32)).astype(bf16)
                out_y[slot, c, lower] = value[half:].astype(bf16)

            def three(c):
                value = block(targets[3], i * ch + c) + in_c[slot, 3, c].astype(f32)
                total[i * ch + c] = value.astype(bf16)

            each(one)
            each(two)
            x_copy(slot).start()
            y_copy(slot).start()
            each(three)

        old = slot_of(i - SUM_LAG)

        @pl.when(inside(i - SUM_LAG))
        def _():
            x_copy(old).wait_recv()
            y_copy(old).wait_recv()

            def one(c):
                at = (i - SUM_LAG) * ch + c
                value = total[at].astype(f32) + in_x[old, c].astype(f32) + in_y[old, c].astype(f32)
                total[at] = value.astype(bf16)

            each(one)

    def along(j):
        even = lax.rem(j, 2) == 0
        rank = jnp.where(even, z, GROUPS - 1 - z)
        down = jnp.where(even, lax.rem(z + GROUPS - 1, GROUPS), lax.rem(z + 1, GROUPS))
        up = jnp.where(even, lax.rem(z + 1, GROUPS), lax.rem(z + GROUPS - 1, GROUPS))
        return rank, (down, s), (up, s)

    def z_copy(name, j):
        _, down, up = along(j)
        span = pl.ds(j * ch, ch)
        if name == "rise":
            return remote(total.at[span], low_in.at[span], up_send.at[j], low_recv.at[j], up)
        if name == "sink":
            return remote(total.at[span], high_in.at[span], up_send.at[j], high_recv.at[j], down)
        if name == "final_down":
            return remote(final.at[span], final.at[span], down_send.at[0, j], final_recv.at[j], down)
        return remote(final.at[span], final.at[span], down_send.at[1, j], final_recv.at[j], up)

    def over_z(i):
        j = i - SUM_LAG

        @pl.when(inside(j))
        def _():
            rank, _, _ = along(j)

            @pl.when(rank == 0)
            def _():
                z_copy("rise", j).start()

            @pl.when(rank == 3)
            def _():
                z_copy("sink", j).start()

        j2 = j - Z_STEP

        @pl.when(jnp.logical_and(inside(j2), along(j2)[0] == 2))
        def _():
            z_copy("sink", j2).wait_recv()

            def one(c):
                at = j2 * ch + c
                total[at] = (total[at].astype(f32) + high_in[at].astype(f32)).astype(bf16)

            each(one)
            z_copy("sink", j2).start()

        j3 = j - 2 * Z_STEP

        @pl.when(jnp.logical_and(inside(j3), along(j3)[0] == 1))
        def _():
            z_copy("rise", j3).wait_recv()
            z_copy("sink", j3).wait_recv()

            def one(c):
                at = j3 * ch + c
                value = total[at].astype(f32) + low_in[at].astype(f32) + high_in[at].astype(f32)
                final[at] = value.astype(bf16)

            each(one)
            z_copy("final_down", j3).start()
            z_copy("final_up", j3).start()

        j4 = j - 3 * Z_STEP

        @pl.when(jnp.logical_and(inside(j4), along(j4)[0] == 2))
        def _():
            z_copy("final_up", j4).wait_recv()
            z_copy("final_up", j4).start()

        j5 = i - Z_LAG

        @pl.when(inside(j5))
        def _():
            rank = along(j5)[0]

            @pl.when(jnp.logical_or(rank == 0, rank == 3))
            def _():
                z_copy("final_up", j5).wait_recv()

            span = pl.ds(j5 * ch, ch)
            pltpu.make_async_copy(final.at[span], grads_ref.at[span], keep_sem.at[j5]).start()

            def one(c):
                at = j5 * ch + c
                value = final[at].astype(f32) * jnp.where(at < count_ref[0], 1.0, 0.0)
                squares[...] = squares[...] + fold(value * value)

            each(one)

    def settle(i):
        n = i - 2
        slot = slot_of(n)
        for item in range(4):

            @pl.when(inside(n + 1 if item == 0 else n))
            def _():
                c_copy(slot, item).wait_send()

        n2 = i - 3
        slot2 = slot_of(n2)

        @pl.when(inside(n2 + 1))
        def _():
            dx_copy(slot2).wait_send()
            dy_copy(slot2).wait_send()

        @pl.when(inside(n2))
        def _():
            x_copy(slot2).wait_send()
            y_copy(slot2).wait_send()

    hooks = {
        0: spread_stage, 3: pass_stage, 6: order_stage, 13: part_stage, 17: cond_stage, 21: row_stage,
    }
    hooks.update({7 + part: functools.partial(ada_stage, part) for part in range(ADA_PARTS)})

    for_sibling(-1)

    def iteration(step, unused):
        i = step - 1
        for_sibling(i + 1)
        for_owners(i)
        over_z(i)
        settle(i)
        for at, stage in hooks.items():
            pl.when(i == at)(stage)
        return unused

    lax.fori_loop(0, chunks + 1 + Z_LAG, iteration, 0)

    square_in[s] = jnp.zeros((8, 128), f32) + jnp.sum(squares[...])
    begin("square")

    cond_gram = jnp.zeros((images, images), f32)
    for o in range(SHARDS):
        cond_gram += nt(cond_ref[o], cond_ref[o])

    def gram(c, value):
        return value + nt(d_blocks_ref[c], d_blocks_ref[c])

    d_gram = lax.fori_loop(0, 6 * NB, gram, jnp.zeros((images, images), f32))
    got("square")
    value = square_in[0]
    for o in range(1, SHARDS):
        value += square_in[o]
    norm_ref[...] = value + jnp.sum(cond_gram * d_gram)

    def finish(j, unused):
        span = pl.ds(j * ch, ch)
        pltpu.make_async_copy(final.at[span], grads_ref.at[span], keep_sem.at[j]).wait()
        rank = along(j)[0]

        @pl.when(rank == 0)
        def _():
            z_copy("rise", j).wait_send()

        @pl.when(rank >= 2)
        def _():
            z_copy("sink", j).wait_send()

        @pl.when(rank == 1)
        def _():
            z_copy("final_down", j).wait_send()

        @pl.when(jnp.logical_or(rank == 1, rank == 2))
        def _():
            z_copy("final_up", j).wait_send()

        return unused

    lax.fori_loop(0, chunks, finish, 0)
    for name in ("d_far", "stat_far", "tok_far", "tok", "d", "stat", "d_more", "stat_more", "part", "pre", "square"):
        for copy in small_copies(name):
            copy.wait_send()


def collect(cap, left_of, right_of, row_of, col_of, count, acts, dmod, ends, stats, times, conds, freq_low, label, own_pre, own_cond,
            row_master, tile_master):
    per = tile_master.shape[0]
    ch = 1
    chunks = cap // ch
    images = GROUPS * SHARDS
    vmem = pl.BlockSpec(memory_space=pltpu.VMEM)
    smem = pl.BlockSpec(memory_space=pltpu.SMEM)
    anywhere = pl.BlockSpec(memory_space=pl.ANY)
    small = 9 + 6 * (SHARDS - 1)
    dma = pltpu.SemaphoreType.DMA

    def blocks(*lead):
        return pltpu.VMEM(lead + (BLK, BLK), bf16)

    return pl.pallas_call(
        functools.partial(collect_body, cap, ch),
        out_shape=[
            jax.ShapeDtypeStruct((per, BLK, BLK), bf16),
            jax.ShapeDtypeStruct((6 * NB, images, BLK), bf16),
            jax.ShapeDtypeStruct(row_master.shape, f32),
            jax.ShapeDtypeStruct((8, 128), f32),
            jax.ShapeDtypeStruct((8, 128), f32),
        ],
        in_specs=[smem] * 5 + [vmem] * 11 + [anywhere],
        out_specs=[anywhere] + [vmem] * 4,
        scratch_shapes=[
            blocks(RING, 4, ch),
            blocks(RING, 4, ch),
            blocks(RING, ch),
            blocks(RING, ch),
            blocks(RING, ch),
            pltpu.VMEM((RING, ch, BLK // 2, BLK), bf16),
            pltpu.VMEM((RING, ch, BLK // 2, BLK), bf16),
            blocks(RING, ch),
            blocks(RING, ch),
            blocks(cap),
            blocks(cap),
            blocks(cap),
            blocks(cap),
            pltpu.VMEM((per // ADA_PARTS, BLK, BLK), f32),
            pltpu.VMEM((per, images, BLK), f32),
            pltpu.VMEM((images * 8 * LANES, 128), bf16),
            pltpu.VMEM((images * 8 * LANES, 128), f32),
            pltpu.VMEM((images * 8, 128), f32),
            pltpu.VMEM((SHARDS, TOKEN_ROWS, 128), bf16),
            pltpu.VMEM((SHARDS, TOKEN_ROWS, 128), bf16),
            pltpu.VMEM((GROUPS, TOKEN_ROWS, 128), f32),
            pltpu.VMEM((TOKEN_ROWS, 128), f32),
            pltpu.VMEM((SHARDS, images, 128), bf16),
            pltpu.VMEM((SHARDS, images, 128), bf16),
            pltpu.VMEM((SHARDS, images, 128), bf16),
            pltpu.VMEM((SHARDS, images, 128), bf16),
            pltpu.VMEM((images, 128), f32),
            pltpu.VMEM((images, 128), f32),
            pltpu.VMEM((24, 128), f32),
            pltpu.VMEM((8, BLK), f32),
            pltpu.VMEM((SHARDS, 8, 128), f32),
            dma((RING, 4)),
            dma((RING, 4)),
            dma((RING, 2)),
            dma((RING,)),
            dma((RING,)),
            dma((RING,)),
            dma((RING,)),
            dma((RING,)),
            dma((RING,)),
            dma((chunks,)),
            dma((chunks,)),
            dma((chunks,)),
            dma((chunks,)),
            dma((2, chunks)),
            dma((chunks,)),
            dma,
            dma((small,)),
            dma((small,)),
        ],
        compiler_params=pltpu.CompilerParams(
            collective_id=100 + cap, has_side_effects=True, vmem_limit_bytes=50 << 20
        ),
        name="collect",
    )(left_of, right_of, row_of, col_of, count, acts, dmod, ends, stats, times, conds, freq_low, label, own_pre, own_cond,
      row_master, tile_master)


def position_table(grid_side, model_width):
    quarter = model_width // 4
    omega = 1.0 / 10000.0 ** (jnp.arange(quarter, dtype=f32) / quarter)
    angle = jnp.arange(grid_side).astype(f32)[:, None] * omega[None, :]
    return jnp.stack([jnp.sin(angle), jnp.cos(angle)])


def time_freq(step_values, freq_width):
    half_width = freq_width // 2
    freqs = jnp.exp(-math.log(10000.0) * jnp.arange(half_width, dtype=f32) / half_width)
    angle_arg = step_values.astype(f32)[:, None] * freqs[None, :]
    return jnp.concatenate([jnp.cos(angle_arg), jnp.sin(angle_arg)], axis=1)


def silu_slope(value):
    gate = jax.nn.sigmoid(value)
    return gate * (1.0 + value * (1.0 - gate))


def blocked(array):
    count = array.shape[0]
    return array.reshape(count, -1, BLK).transpose(1, 0, 2)


def factors_of(block):
    n = jnp.maximum(block - ADA, 0)
    out, up, down = n - AT_OUT, n - AT_UP, n - AT_DOWN
    row = lax.div(n, jnp.int32(QB))
    left = jnp.where(n < AT_OUT, L_ATT + row, jnp.where(n < AT_UP, L_OUT + (out >> 2), jnp.where(n < AT_DOWN, L_MLP + (up >> 4), L_HID + (down >> 2))))
    right = jnp.where(
        n < AT_OUT,
        R_QKV + n - row * QB,
        jnp.where(n < AT_UP, R_OUT + (out & (NB - 1)), jnp.where(n < AT_DOWN, R_UP + (up & (HB - 1)), R_DOWN + (down & (NB - 1)))),
    )
    return left, right


def places_body(
    per, assign_ref, slot_ref, row_ref, col_ref, rank_ref, inverse_ref, left_ref, right_ref, count_ref, tier_ref
):
    me = lax.axis_index("shard")

    def place_in(block, s, before):
        return jnp.where(block < ADA, per - 1 - (s - before), before), before + jnp.where(block < ADA, 0, 1)

    def owner(o, most):
        def slot(s, before):
            block = assign_ref[o * per + s]
            p, after = place_in(block, s, before)
            place = o * per + p
            inverse_ref[block] = place
            left, right = factors_of(block)
            left_ref[place] = left
            right_ref[place] = right
            return after

        return jnp.maximum(most, lax.fori_loop(0, per, slot, jnp.int32(0), unroll=True))

    most = lax.fori_loop(0, assign_ref.shape[0] // per, owner, jnp.int32(0))
    tier_ref[0] = sum(jnp.where(most > cap, 1, 0) for cap in CAPS)

    def own(s, before):
        block = assign_ref[me * per + s]
        p, after = place_in(block, s, before)
        slot_ref[p] = s
        rank_ref[s] = p
        row_ref[s] = jnp.where(block < ADA, block // (6 * NB), 0)
        col_ref[s] = jnp.where(block < ADA, block % (6 * NB), -1)
        return after

    count_ref[0] = lax.fori_loop(0, per, own, jnp.int32(0), unroll=True)


def find_places(assign, per):
    smem = pl.BlockSpec(memory_space=pltpu.SMEM)

    def ints(count):
        return jax.ShapeDtypeStruct((count,), jnp.int32)

    total = assign.shape[0]
    return pl.pallas_call(
        functools.partial(places_body, per),
        out_shape=[ints(per)] * 4 + [ints(total)] * 3 + [ints(1)] * 2,
        in_specs=[smem],
        out_specs=[smem] * 9,
        name="find_places",
    )(assign)


def spread_plain(slot_of, row_of, col_of, tile_master, row_master, timesteps, labels):
    shard_count = lax.axis_size("shard")
    everyone = ("grp", "shard")
    me = lax.axis_index("shard")
    per, columns = tile_master.shape[0], row_master.shape[1]
    low_rows = row_master.astype(bf16)
    at = [0]

    def take(count):
        at[0] += count
        return low_rows[at[0] - count : at[0]]

    table, w_time1, w_time2 = take(NCLASS), take(FREQ), take(D)
    w_final = (take(D), take(D))
    take(2 * PATCH_DIM)
    take(1)
    b_time1, b_time2 = take(1), take(1)
    take(4)
    b_ada = take(6)
    take(FF // D)
    b_final = take(2)
    b_mod = jnp.concatenate([b_ada, b_final], axis=0)

    packed = pack_tiles(slot_of, tile_master)
    gathered = lax.all_gather(packed, "shard", axis=0, tiled=True)
    near = lax.all_gather(low_rows[NEAR_START:], "shard", axis=1, tiled=True)
    near = jnp.pad(near, ((0, NEAR - NEAR_REAL), (0, 0))).reshape(NEAR, LANES, 128).transpose(1, 0, 2)

    ids = lax.all_gather(jnp.concatenate([timesteps, labels]), everyone, axis=0)
    all_steps, all_labels = ids[:, 0], ids[:, 1]
    freq_low = time_freq(all_steps, FREQ).astype(bf16)
    own_pre = nn(freq_low, w_time1) + b_time1
    time_low = lax.all_gather(jax.nn.silu(own_pre).astype(bf16), "shard", axis=1, tiled=True)
    one_hot = (all_labels[:, None] == jnp.arange(NCLASS, dtype=jnp.int32)[None, :]).astype(bf16)
    own_cond = nn(time_low, w_time2) + b_time2 + nn(one_hot, table)
    cond_low = lax.all_gather(jax.nn.silu(own_cond).astype(bf16), "shard", axis=1, tiled=True)
    group_cond = lax.dynamic_slice(cond_low, (lax.axis_index("grp") * shard_count, 0), (shard_count, D))
    part_mod = ada_front(row_of, col_of, blocked(group_cond), tile_master)
    part_mod = part_mod.transpose(1, 0, 2).reshape(shard_count, 6, D)
    part_final = jnp.stack([nn(group_cond, w_final[0]), nn(group_cond, w_final[1])], axis=1)
    spread = jnp.zeros((shard_count, 8, D), f32)
    spread = lax.dynamic_update_slice(
        spread,
        jnp.concatenate([jnp.zeros((shard_count, 6, columns), f32), part_final], axis=1) + b_mod[None].astype(f32),
        (0, 0, me * columns),
    )
    spread = spread + jnp.concatenate([part_mod, jnp.zeros((shard_count, 2, D), f32)], axis=1)
    mods = lax.psum_scatter(spread, "shard", scatter_dimension=0, tiled=True)[0]
    label = jnp.broadcast_to(all_labels.astype(f32)[:, None], (all_labels.shape[0], 128))

    def lanes(array):
        return array.reshape(-1, LANES, 128).transpose(1, 0, 2)

    return (
        gathered, near, mods.reshape(8 * LANES, 128), freq_low, label, lanes(time_low), lanes(cond_low), own_pre, own_cond,
    )


def collect_plain(left_of, right_of, row_of, col_of, count, acts, dmod, ends, stats, times, conds, freq_low, label, own_pre, own_cond,
                  row_master, tile_master):
    everyone = ("grp", "shard")
    me = lax.axis_index("shard")
    columns = row_master.shape[1]
    low_rows = row_master.astype(bf16)
    w_time2 = low_rows[NCLASS + FREQ : NCLASS + FREQ + D]
    w_final = [low_rows[NCLASS + FREQ + (1 + i) * D : NCLASS + FREQ + (2 + i) * D] for i in range(2)]
    one_hot = (label[:, :1].astype(jnp.int32) == jnp.arange(NCLASS, dtype=jnp.int32)[None, :]).astype(bf16)
    time_low, cond_low = (array.transpose(1, 0, 2).reshape(-1, D) for array in (times, conds))
    partial = tile_grads(left_of, right_of, acts)
    own_tiles = lax.psum_scatter(partial, "shard", scatter_dimension=0, tiled=True)
    own_tiles = lax.psum(own_tiles, "grp")

    all_dmod = lax.all_gather(dmod.reshape(1, -1).astype(bf16), everyone, axis=0, tiled=True)
    dmod_blocks = blocked(all_dmod[:, : 6 * D])
    own_dmod = lax.dynamic_slice(all_dmod.reshape(-1, 8, D), (0, 0, me * columns), (all_dmod.shape[0], 8, columns))
    part_cond = ada_back(row_of, col_of, dmod_blocks, tile_master).transpose(1, 0, 2).reshape(-1, D)
    part_cond = part_cond + nt(own_dmod[:, 6], w_final[0]) + nt(own_dmod[:, 7], w_final[1])
    own_dcond = lax.psum_scatter(part_cond, "shard", scatter_dimension=1, tiled=True) * silu_slope(own_cond)
    dcond_low = own_dcond.astype(bf16)
    own_dpre = lax.psum_scatter(nt(dcond_low, w_time2), "shard", scatter_dimension=1, tiled=True)
    own_dpre = own_dpre * silu_slope(own_pre)
    wide_dmod = own_dmod.astype(f32)

    token_rows = ends.transpose(1, 0, 2).reshape(TOKEN_ROWS, D)
    token_rows = lax.psum_scatter(token_rows, "shard", scatter_dimension=1, tiled=True)
    token_rows = lax.psum(token_rows, "grp")
    own_rows = jnp.concatenate(
        [
            tn(one_hot.astype(f32), own_dcond),
            tn(freq_low, own_dpre.astype(bf16)),
            tn(time_low, dcond_low),
            tn(cond_low, own_dmod[:, 6]),
            tn(cond_low, own_dmod[:, 7]),
            token_rows[: T_PATCH + 1],
            jnp.sum(own_dpre, axis=0)[None],
            jnp.sum(own_dcond, axis=0)[None],
            token_rows[T_QUERY : T_VALUE + 1],
            token_rows[T_OUT : T_DOWN + 1],
            jnp.sum(wide_dmod[:, :6], axis=0),
            token_rows[T_UP:T_END],
            jnp.sum(wide_dmod[:, 6:], axis=0),
        ],
        axis=0,
    )
    totals = lax.psum(stats, everyone)
    cond_gram = nt(cond_low, cond_low)
    dmod_gram = nt(all_dmod[:, : 6 * D], all_dmod[:, : 6 * D])
    counted = jnp.arange(own_tiles.shape[0], dtype=jnp.int32) < count
    wide_tiles = jnp.where(counted[:, None, None], own_tiles.astype(f32), 0.0)
    square_part = jnp.sum(wide_tiles * wide_tiles) + jnp.sum(own_rows * own_rows)
    square_sum = lax.psum(square_part, "shard") + jnp.sum(cond_gram * dmod_gram)
    return own_tiles, dmod_blocks, own_rows, jnp.broadcast_to(square_sum, (8, 128)), totals


def pack_body(slot_ref, tile_ref, out_ref):
    out_ref[...] = tile_ref[...].astype(bf16)


def pack_tiles(slot_of, tile_master):
    per = tile_master.shape[0]
    return pl.pallas_call(
        pack_body,
        grid_spec=pltpu.PrefetchScalarGridSpec(
            num_scalar_prefetch=1,
            grid=(per,),
            in_specs=[pl.BlockSpec((1, BLK, BLK), lambda p, slots: (slots[p], 0, 0))],
            out_specs=pl.BlockSpec((1, BLK, BLK), lambda p, slots: (p, 0, 0)),
        ),
        out_shape=jax.ShapeDtypeStruct(tile_master.shape, bf16),
        name="pack_tiles",
    )(slot_of, tile_master)


def shards(
    patches, noise, timesteps, labels, assign, tile_master, tile_bases, tile_moment, tile_second,
    row_master, row_moment, row_second,
):
    group_count, shard_count = lax.axis_size("grp"), lax.axis_size("shard")
    everyone = ("grp", "shard")
    me = lax.axis_index("shard")
    per = tile_master.shape[0]
    columns = row_master.shape[1]
    token_total = patches.shape[0] * group_count * shard_count
    tile_total = assign.shape[0]

    slot_of, row_of, col_of, rank, inverse, left_of, right_of, count, tier = find_places(assign, per)
    fast = group_count == GROUPS and shard_count == SHARDS
    if fast:
        tier = tier[0]
        gathered, near, mods, freq_low, label, times, conds, own_pre, own_cond = lax.switch(
            tier, [functools.partial(spread, cap) for cap in CAPS + (per,)], slot_of, row_of, col_of, timesteps, labels, tile_master, row_master,
        )
        gathered = gathered.reshape(tile_total, BLK, BLK)
    else:
        gathered, near, mods, freq_low, label, times, conds, own_pre, own_cond = spread_plain(
            slot_of, row_of, col_of, tile_master, row_master, timesteps, labels
        )

    loss_scale = 1.0 / (token_total * PATCH_DIM)
    acts, dmod, ends, stats = block_step(
        inverse, gathered, patches.T, noise.T, position_table(LAT // PATCH_SIDE, D), near, mods.reshape(8 * LANES, 128),
        2.0 * loss_scale,
    )

    if fast:
        own_tiles, dmod_blocks, own_rows, squares, totals = lax.switch(
            tier, [functools.partial(collect, cap) for cap in CAPS + (per,)], left_of, right_of, row_of, col_of, count, acts, dmod, ends, stats, times, conds, freq_low, label, own_pre,
            own_cond, row_master, tile_master,
        )
    else:
        own_tiles, dmod_blocks, own_rows, squares, totals = collect_plain(
            left_of, right_of, row_of, col_of, count, acts, dmod, ends, stats, times, conds, freq_low, label, own_pre,
            own_cond, row_master, tile_master,
        )
    new_tile_moment, new_tile_second, tile_update, new_row_moment, new_row_second, row_update, loss, grad_norm, act_rms = adam(
        (1.0 / (token_total * PATCH_DIM), 1.0 / (token_total * D)), rank, row_of, col_of, squares, totals, own_tiles, conds,
        dmod_blocks, tile_bases, tile_moment, tile_second, own_rows, row_master, row_moment, row_second,
    )
    loss, grad_norm = loss.reshape(()), grad_norm.reshape(())
    return (
        loss, grad_norm, act_rms, new_tile_moment, new_tile_second, tile_update, new_row_moment, new_row_second, row_update,
    )


def solution(mesh):
    placed = (
        P(("grp", "shard"), None),
        P(("grp", "shard"), None),
        P(("grp", "shard")),
        P(("grp", "shard")),
        P(),
        P("shard", None, None),
        P("shard", None, None, None),
        P("shard", None, None),
        P("shard", None, None),
        P(None, "shard"),
        P(None, "shard"),
        P(None, "shard"),
    )
    return jax.shard_map(
        shards,
        mesh=mesh,
        in_specs=placed,
        out_specs=(
            P(), P(), P(),
            P("shard", None, None), P("shard", None, None), P("shard", None, None),
            P(None, "shard"), P(None, "shard"), P(None, "shard"),
        ),
        check_vma=False,
    )
```

profile of v0, /device:TPU:0, one launch (start us, length us, event | category | flops | bytes accessed | tf_op | source)
XLA Modules:
  0.0 367.8 jit_solution(670699575204629052)
XLA Ops:
  0.6 5.5 %find_places.1 = (s32[36]{0:T(128)S(1)}, s32[36]{0:T(128)S(1)}, s32[36]{0:T(128)S(1)}, s32[36]{0:T(128)}, s32[288]{0:T(512)}, /*index=5*/s32[288]{0:T(512)S(1)}, s32[288]{0:T(512)S(1)}, s32[1]{0:T(128)}, s32[1]{0:T(128)}) custom-call(s32[288]{0:T(512)} %assign_ref.1), custom_call_target="tpu_custom_call" | custom-call | tf_op jit(solution)/shard_map/find_places/pallas_call | solution.py:1646
  6.8 105.5 %conditional.2 = ((bf16[8,36,256,256]{3,2,1,0:T(8,128)(2,1)}, bf16[8,64,128]{2,1,0:T(8,128)(2,1)S(1)}, f32[64,128]{1,0:T(8,128)S(1)}, bf16[32,256]{1,0:T(8,128)(...) conditional(s32[]{:T(128)} %bitcast, (s32[36]{0:T(128)S(1)}, ...), branch_computations={%region_0.0_spmd, %region_1.0_spmd, %region_2.0_spmd} | conditional | bytes 8 | solution.py:1804
  6.8 105.2 %spread.3 = (bf16[8,36,256,256]{3,2,1,0:T(8,128)(2,1)}, bf16[8,64,128]{2,1,0:T(8,128)(2,1)S(1)}, f32[64,128]{1,0:T(8,128)S(1)}, bf16[32,256]{1,0:T(8,128)(2,1)S(...) custom-call(s32[36]{0:T(128)S(1)} %get-tuple-element.182.slot_ref, ...), custom_call_target="tpu_custom_call" | custom-call | tf_op jit(solution)/shard_map/cond/branch_0_fun/spread/pallas_call | solution.py:901
  112.3 0.1 multiply_sine_fusion
  112.5 0.6 pad_maximum_fusion.spot_ref
  113.1 0.0 copy-start
  113.1 45.1 %block_step.1 = (bf16[64,256,256]{2,1,0:T(8,128)(2,1)}, f32[64,128]{1,0:T(8,128)S(1)}, f32[8,48,128]{2,1,0:T(8,128)S(1)}, f32[8,128]{1,0:T(8,128)S(1)}) custom-call(s32[288]{0:T(512)} %get-tuple-element.306.place_ref, bf16[288,256,256]{2,1,0:T(8,128)(2,1)} %bitcast.6, bf16[16,256]{1,0:T(8,128)(2,1)} %bitcast.8, f32[16,256]{1,0:T(8,128)} %bitcast.7, ...), custom_call_target="tpu_custom_call" | custom-call | flops 19327352832 | bytes 50331648 | tf_op jit(solution)/shard_map/block_step/pallas_call | solution.py:424
  158.2 0.0 copy-done
  158.3 173.8 %conditional.3 = ((bf16[36,256,256]{2,1,0:T(8,128)(2,1)}, bf16[24,32,256]{2,1,0:T(8,128)(2,1)S(1)}, f32[4379,128]{1,0:T(8,128)}, f32[8,128]{1,0:T(8,128)S(1)}, f32[8,128]{1,0:T(8,128)S(1)})) conditional(s32[]{:T(128)} %bitcast, (s32[288]{0:T(512)S(1)}, s32[288]{0:T(512)S(1)}, s32[36]{0:T(128)S(1)}, s32[36]{0:T(128)S(1)}, ...), branch_computations={%region_3.0_spmd, %region_4.0_spmd, %region_5.0_spmd} | conditional | bytes 8 | solution.py:1820
  170.5 161.6 %collect.3 = (bf16[36,256,256]{2,1,0:T(8,128)(2,1)}, bf16[24,32,256]{2,1,0:T(8,128)(2,1)S(1)}, f32[4379,128]{1,0:T(8,128)}, f32[8,128]{1,0:T(8,128)S(1)}, f32[8,128]{1,0:T(8,128)S(1)}) custom-call(s32[288]{0:T(512)S(1)} %get-tuple-element.203.left_ref, s32[288]{0:T(512)S(1)} %get-tuple-element.204.right_ref, s32[36]{0:T(128)S(1)} %get-tuple-element.205.row_ref, ...), custom_call_target="tpu_custom_call" | custom-call | tf_op jit(solution)/shard_map/cond/branch_0_fun/collect/pallas_call | solution.py:1496
  332.1 35.5 %adam.1 = (f32[36,256,256]{2,1,0:T(8,128)}, f32[36,256,256]{2,1,0:T(8,128)}, f32[36,256,256]{2,1,0:T(8,128)}, f32[4379,128]{1,0:T(8,128)}, f32[4379,128]{1,0:T(8...) custom-call(s32[36]{0:T(128)} %get-tuple-element.299.where_ref, ...), custom_call_target="tpu_custom_call" | custom-call | tf_op jit(solution)/shard_map/adam/pallas_call | solution.py:599
  (2 shorter events, 0.0 us)
Async XLA Ops:
  113.1 45.1 %copy-start = (f32[36,256,256]{2,1,0:T(8,128)S(1)}, f32[36,256,256]{2,1,0:T(8,128)}, u32[]{:S(2)}) copy-start(f32[36,256,256]{2,1,0:T(8,128)} %param.23) | copy-start | bytes 28311556
where the time goes:
time: 369 us; the launch traced here: 368 us
  Pallas kernels  353 us (96%)
  loops' own time  12.5 us (3%)
    pallas_call x1, Pallas kernels, collect(): pl.pallas_call(functools.partial(collect_body, cap, ch), out_shape=[jax.S...  162 us
    pallas_call x1, Pallas kernels, spread(): pl.pallas_call(functools.partial(spread_body, cap, n_third), out_shape=[j...  105 us
    pallas_call x1, Pallas kernels, block_step(): pl.pallas_call(functools.partial(block_body, loss_factor), out_shape=[jax...  45.1 us
    pallas_call x1, Pallas kernels, adam(): pl.pallas_call(functools.partial(adam_body, group, factors), grid_spec=pl...  35.5 us
    another operation x1, loops' own time, shards(): lax.switch(tier, [functools.partial(collect, cap) for cap in CAPS + (per,...  12.2 us

commit v1 on v0

--- a/solution.py
+++ b/solution.py
@@ -625,10 +625,10 @@
 
 def spread_body(
     cap, n_third,
-    slot_ref, row_ref, col_ref, step_ref, name_ref, tiles_ref, rows_ref,
-    out_ref, near_ref, mods_ref, freq_ref, label_ref, time_ref, cond_ref, pre_ref, own_cond_ref,
-    tile, pack, ids, near, times, conds, near_wide, cond_group, product, part, part_out, part_in,
-    load_sem, keep_sem, send_sem, recv_sem, small_send, small_recv,
+    slot_ref, row_ref, col_ref, step_ref, name_ref, tiles_ref, bases_ref, rows_ref,
+    out_ref, bases_low_ref, near_ref, mods_ref, freq_ref, label_ref, time_ref, cond_ref, pre_ref, own_cond_ref,
+    tile, pack, ids, near, times, conds, near_wide, cond_group, product, part, part_out, part_in, basis, basis_low,
+    basis_sem, basis_low_sem, load_sem, keep_sem, send_sem, recv_sem, small_send, small_recv,
 ):
     z, s = lax.axis_index("grp"), lax.axis_index("shard")
     per = tile.shape[0]
@@ -795,8 +795,11 @@
             cond_group[o // 2, :, half * 128 : (half + 1) * 128] = nn(pick, conds[o])
 
     def ada_stage(start, count):
-        for j in range(start, start + count):
+        def one(j, unused):
             product[j] = nn(cond_group[row_ref[j]].astype(bf16), tile[j].astype(bf16))
+            return unused
+
+        lax.fori_loop(start, start + count, one, 0)
 
     def part_stage():
         part[...] = jnp.zeros_like(part)
@@ -835,6 +838,39 @@
         time_ref[...] = times[...]
         cond_ref[...] = conds[...]
 
+    pieces = per // basis.shape[1]
+
+    def basis_load(k):
+        span = pl.ds(k * basis.shape[1], basis.shape[1])
+        return pltpu.make_async_copy(bases_ref.at[span], basis.at[k % 2], basis_sem.at[k % 2])
+
+    def basis_store(k):
+        span = pl.ds(k * basis.shape[1], basis.shape[1])
+        return pltpu.make_async_copy(basis_low.at[k % 2], bases_low_ref.at[span], basis_low_sem.at[k % 2])
+
+    taken = [0]
+
+    def narrow():
+        k = taken[0]
+        if k == pieces:
+            return
+        taken[0] += 1
+        basis_load(k).wait()
+        if k >= 2:
+            basis_store(k - 2).wait()
+        def one(i, unused):
+            for side in range(2):
+                basis_low[k % 2, i, side] = basis[k % 2, i, side].astype(bf16)
+            return unused
+
+        lax.fori_loop(0, basis.shape[1], one, 0)
+        basis_store(k).start()
+        if k + 2 < pieces:
+            basis_load(k + 2).start()
+
+    basis_load(0).start()
+    basis_load(1).start()
+
     cut = per // 3
     hooks = [
         (0.10, time_stage), (0.30, cond_stage), (0.50, group_stage), (0.55, lambda: ada_stage(0, cut)),
@@ -845,6 +881,7 @@
 
     def hook(last=False):
         steps[0] += 1
+        narrow()
         while hooks and (last or steps[0] >= hooks[0][0] * 3 * n_third):
             hooks.pop(0)[1]()
 
@@ -881,6 +918,10 @@
     while seen[0] < 3 * n_third:
         z_next()
     hook(last=True)
+    while taken[0] < pieces:
+        narrow()
+    for k in range(pieces - 2, pieces):
+        basis_store(k).wait()
     for index in range(3 * n_third):
         wait_for(3, index, s ^ 1)
         for which in range(3):
@@ -890,7 +931,7 @@
         copy.wait_send()
 
 
-def spread(cap, slot_of, row_of, col_of, timesteps, labels, tile_master, row_master):
+def spread(cap, slot_of, row_of, col_of, timesteps, labels, tile_master, tile_bases, row_master):
     per = tile_master.shape[0]
     n_third = 5
     images = GROUPS * SHARDS
@@ -898,10 +939,12 @@
     smem = pl.BlockSpec(memory_space=pltpu.SMEM)
     anywhere = pl.BlockSpec(memory_space=pl.ANY)
     small = (GROUPS - 1) + 5 * (SHARDS - 1)
+    few = per // 12
     return pl.pallas_call(
         functools.partial(spread_body, cap, n_third),
         out_shape=[
             jax.ShapeDtypeStruct((SHARDS, per, BLK, BLK), bf16),
+            jax.ShapeDtypeStruct(tile_bases.shape, bf16),
             jax.ShapeDtypeStruct((LANES, NEAR, 128), bf16),
             jax.ShapeDtypeStruct((8 * LANES, 128), f32),
             jax.ShapeDtypeStruct((images, FREQ), bf16),
@@ -911,8 +954,8 @@
             jax.ShapeDtypeStruct((images, 128), f32),
             jax.ShapeDtypeStruct((images, 128), f32),
         ],
-        in_specs=[smem] * 5 + [anywhere, vmem],
-        out_specs=[anywhere] + [vmem] * 8,
+        in_specs=[smem] * 5 + [anywhere, anywhere, vmem],
+        out_specs=[anywhere] * 2 + [vmem] * 8,
         scratch_shapes=[
             pltpu.VMEM((per, BLK, BLK), f32),
             pltpu.VMEM((cap, BLK, BLK), bf16),
@@ -926,6 +969,10 @@
             pltpu.VMEM((8 * LANES * 8, 128), f32),
             pltpu.VMEM((SHARDS, 8 * LANES, 128), f32),
             pltpu.VMEM((SHARDS, 8 * LANES, 128), f32),
+            pltpu.VMEM((2, few, 2, BLK, BLK), f32),
+            pltpu.VMEM((2, few, 2, BLK, BLK), bf16),
+            pltpu.SemaphoreType.DMA((2,)),
+            pltpu.SemaphoreType.DMA((2,)),
             pltpu.SemaphoreType.DMA,
             pltpu.SemaphoreType.DMA,
             pltpu.SemaphoreType.DMA((11, 3 * n_third)),
@@ -935,7 +982,7 @@
         ],
         compiler_params=pltpu.CompilerParams(collective_id=cap, has_side_effects=True, vmem_limit_bytes=61 << 20),
         name="spread",
-    )(slot_of, row_of, col_of, timesteps, labels, tile_master, row_master)
+    )(slot_of, row_of, col_of, timesteps, labels, tile_master, tile_bases, row_master)
 
 RING = 6
 SUM_LAG = 2
@@ -1097,10 +1144,15 @@
         count = tile.shape[0]
         load(part).wait()
 
-        for j in range(count):
+        def one(j, unused):
             at = part * count + j
             product[at] = nt(d_blocks_ref[jnp.maximum(col_ref[at], 0)], tile[j].astype(bf16))
-        if (part + 1) * count < per:
+            return unused
+
+        lax.fori_loop(0, count, one, 0)
+
+        @pl.when(part < ADA_PARTS - 1)
+        def _():
             load(part + 1).start()
 
     def row_slice(start, count):
@@ -1416,7 +1468,6 @@
     hooks = {
         0: spread_stage, 3: pass_stage, 6: order_stage, 13: part_stage, 17: cond_stage, 21: row_stage,
     }
-    hooks.update({7 + part: functools.partial(ada_stage, part) for part in range(ADA_PARTS)})
 
     for_sibling(-1)
 
@@ -1426,6 +1477,7 @@
         for_owners(i)
         over_z(i)
         settle(i)
+        pl.when(jnp.logical_and(i >= 7, i < 7 + ADA_PARTS))(lambda: ada_stage(i - 7))
         for at, stage in hooks.items():
             pl.when(i == at)(stage)
         return unused
@@ -1601,7 +1653,7 @@
 
 
 def places_body(
-    per, assign_ref, slot_ref, row_ref, col_ref, rank_ref, inverse_ref, left_ref, right_ref, count_ref, tier_ref
+    per, assign_ref, left_table, right_table, slot_ref, row_ref, col_ref, rank_ref, inverse_ref, left_ref, right_ref, count_ref, tier_ref
 ):
     me = lax.axis_index("shard")
 
@@ -1614,9 +1666,8 @@
             p, after = place_in(block, s, before)
             place = o * per + p
             inverse_ref[block] = place
-            left, right = factors_of(block)
-            left_ref[place] = left
-            right_ref[place] = right
+            left_ref[place] = left_table[block]
+            right_ref[place] = right_table[block]
             return after
 
         return jnp.maximum(most, lax.fori_loop(0, per, slot, jnp.int32(0), unroll=True))
@@ -1646,10 +1697,10 @@
     return pl.pallas_call(
         functools.partial(places_body, per),
         out_shape=[ints(per)] * 4 + [ints(total)] * 3 + [ints(1)] * 2,
-        in_specs=[smem],
+        in_specs=[smem] * 3,
         out_specs=[smem] * 9,
         name="find_places",
-    )(assign)
+    )(assign, *factors_of(jnp.arange(total, dtype=jnp.int32)))
 
 
 def spread_plain(slot_of, row_of, col_of, tile_master, row_master, timesteps, labels):
@@ -1801,11 +1852,13 @@
     fast = group_count == GROUPS and shard_count == SHARDS
     if fast:
         tier = tier[0]
-        gathered, near, mods, freq_low, label, times, conds, own_pre, own_cond = lax.switch(
-            tier, [functools.partial(spread, cap) for cap in CAPS + (per,)], slot_of, row_of, col_of, timesteps, labels, tile_master, row_master,
+        gathered, bases, near, mods, freq_low, label, times, conds, own_pre, own_cond = lax.switch(
+            tier, [functools.partial(spread, cap) for cap in CAPS + (per,)], slot_of, row_of, col_of, timesteps, labels,
+            tile_master, tile_bases, row_master,
         )
         gathered = gathered.reshape(tile_total, BLK, BLK)
     else:
+        bases = tile_bases
         gathered, near, mods, freq_low, label, times, conds, own_pre, own_cond = spread_plain(
             slot_of, row_of, col_of, tile_master, row_master, timesteps, labels
         )
@@ -1828,7 +1881,7 @@
         )
     new_tile_moment, new_tile_second, tile_update, new_row_moment, new_row_second, row_update, loss, grad_norm, act_rms = adam(
         (1.0 / (token_total * PATCH_DIM), 1.0 / (token_total * D)), rank, row_of, col_of, squares, totals, own_tiles, conds,
-        dmod_blocks, tile_bases, tile_moment, tile_second, own_rows, row_master, row_moment, row_second,
+        dmod_blocks, bases, tile_moment, tile_second, own_rows, row_master, row_moment, row_second,
     )
     loss, grad_norm = loss.reshape(()), grad_norm.reshape(())
     return (

time: 369 us -> 353 us (0.957)
  loops' own time: 12.5 us -> 0.45 us
  Pallas kernels: 353 us -> 349 us
    another operation x1, loops' own time: 12.2 us -> 0.24 us  [shards(): lax.switch(tier, [functools.partial(collect, cap) for cap in CAPS + (per,...]
where the time goes in v1:
time: 353 us; the launch traced here: 352 us
  Pallas kernels  349 us (99%)
    pallas_call x1, Pallas kernels, collect(): pl.pallas_call(functools.partial(collect_body, cap, ch), out_shape=[jax.S...  162 us
    pallas_call x1, Pallas kernels, spread(): pl.pallas_call(functools.partial(spread_body, cap, n_third), out_shape=[j...  105 us
    pallas_call x1, Pallas kernels, block_step(): pl.pallas_call(functools.partial(block_body, loss_factor), out_shape=[jax...  45.1 us
    pallas_call x1, Pallas kernels, adam(): pl.pallas_call(functools.partial(adam_body, group, factors), grid_spec=pl...  34 us

profile of v1, /device:TPU:0, one launch (start us, length us, event | category | flops | bytes accessed | tf_op | source)
XLA Modules:
  0.0 352.4 jit_solution(14389383005493841907)
XLA Ops:
  0.6 0.6 select_select_fusion
  1.2 3.2 find_places.1
  5.1 105.5 %conditional.2 = ((bf16[8,36,256,256]{3,2,1,0:T(8,128)(2,1)}, bf16[36,2,256,256]{3,2,1,0:T(8,128)(2,1)}, bf16[8,64,128]{2,1,0:T(8,128)(2,1)S(1)}, f32[64,128]{1,...) conditional(s32[]{:T(128)} %bitcast, (s32[36]{0:T(128)S(1)}, ...), branch_computations={%region_0.1_spmd, %region_1.2_spmd, %region_2.3_spmd} | conditional | bytes 8 | solution.py:1855
  5.1 105.2 %spread.3 = (bf16[8,36,256,256]{3,2,1,0:T(8,128)(2,1)}, bf16[36,2,256,256]{3,2,1,0:T(8,128)(2,1)}, bf16[8,64,128]{2,1,0:T(8,128)(2,1)S(1)}, f32[64,128]{1,0:T(8,...) custom-call(s32[36]{0:T(128)S(1)} %get-tuple-element.192.slot_ref, ...), custom_call_target="tpu_custom_call" | custom-call | tf_op jit(solution)/shard_map/cond/branch_0_fun/spread/pallas_call | solution.py:943
  110.5 0.1 multiply_sine_fusion
  110.7 0.6 pad_maximum_fusion.spot_ref
  111.3 0.0 copy-start
  111.3 45.1 %block_step.1 = (bf16[64,256,256]{2,1,0:T(8,128)(2,1)}, f32[64,128]{1,0:T(8,128)S(1)}, f32[8,48,128]{2,1,0:T(8,128)S(1)}, f32[8,128]{1,0:T(8,128)S(1)}) custom-call(s32[288]{0:T(512)} %get-tuple-element.320.place_ref, bf16[288,256,256]{2,1,0:T(8,128)(2,1)} %bitcast.6, bf16[16,256]{1,0:T(8,128)(2,1)} %bitcast.8, f32[16,256]{1,0:T(8,128)} %bitcast.7, ...), custom_call_target="tpu_custom_call" | custom-call | flops 19327352832 | bytes 50331648 | tf_op jit(solution)/shard_map/block_step/pallas_call | solution.py:424
  156.5 0.0 copy-done
  156.5 161.8 %conditional.3 = ((bf16[36,256,256]{2,1,0:T(8,128)(2,1)}, bf16[24,32,256]{2,1,0:T(8,128)(2,1)S(1)}, f32[4379,128]{1,0:T(8,128)}, f32[8,128]{1,0:T(8,128)S(1)}, f32[8,128]{1,0:T(8,128)S(1)})) conditional(s32[]{:T(128)} %bitcast, (s32[288]{0:T(512)S(1)}, s32[288]{0:T(512)S(1)}, s32[36]{0:T(128)S(1)}, s32[36]{0:T(128)S(1)}, ...), branch_computations={%region_3.4_spmd, %region_4.5_spmd, %region_5.6_spmd} | conditional | bytes 8 | solution.py:1873
  156.7 161.5 %collect.3 = (bf16[36,256,256]{2,1,0:T(8,128)(2,1)}, bf16[24,32,256]{2,1,0:T(8,128)(2,1)S(1)}, f32[4379,128]{1,0:T(8,128)}, f32[8,128]{1,0:T(8,128)S(1)}, f32[8,128]{1,0:T(8,128)S(1)}) custom-call(s32[288]{0:T(512)S(1)} %get-tuple-element.216.left_ref, s32[288]{0:T(512)S(1)} %get-tuple-element.217.right_ref, s32[36]{0:T(128)S(1)} %get-tuple-element.218.row_ref, ...), custom_call_target="tpu_custom_call" | custom-call | tf_op jit(solution)/shard_map/cond/branch_0_fun/collect/pallas_call | solution.py:1548
  318.2 34.0 %adam.1 = (f32[36,256,256]{2,1,0:T(8,128)}, f32[36,256,256]{2,1,0:T(8,128)}, f32[36,256,256]{2,1,0:T(8,128)}, f32[4379,128]{1,0:T(8,128)}, f32[4379,128]{1,0:T(8...) custom-call(s32[36]{0:T(128)} %get-tuple-element.313.where_ref, ...), custom_call_target="tpu_custom_call" | custom-call | tf_op jit(solution)/shard_map/adam/pallas_call | solution.py:599
  (2 shorter events, 0.0 us)
Async XLA Ops:
  111.3 45.1 %copy-start = (f32[36,256,256]{2,1,0:T(8,128)S(1)}, f32[36,256,256]{2,1,0:T(8,128)}, u32[]{:S(2)}) copy-start(f32[36,256,256]{2,1,0:T(8,128)} %param.23) | copy-start | bytes 28311556
